TPU v7x, 32 devices: a whole 2x2x4 slice. The times are simulated.
32 devices in a mesh: dom: 4 (over y, core), seq: 8 (over z, x).
Axes of the slice: x: 2, y: 2, z: 4, core: 2. Of those that a mesh axis runs over, the one named last changes fastest.
Arguments:
- tokens_x: bfloat16 [8192, 4096], P(('dom', 'seq')), may hold values from -6 to 6
- gate_z: bfloat16 [8192, 4096], P(('dom', 'seq')), may hold values from -6 to 6
- in_b: bfloat16 [8192, 128], P(('dom', 'seq')), may hold values from -6 to 6
- in_c: bfloat16 [8192, 128], P(('dom', 'seq')), may hold values from -0.19921875 to 0.19921875
- log_decay: bfloat16 [8192, 64], P(('dom', 'seq')), may hold values from -1 to 0
- domain_ids: int32 [4, 8, 4], P('dom', 'seq'), may hold values from 0 to 3, each once within a row
- out_weight: bfloat16 [4, 4096, 4096], P('dom', None, 'seq'), may hold values from -0.09375 to 0.09375
- norm_gain: float32 [4, 4096], P('dom'), may hold values from 0.1 to 1.9
- skip_gain: float32 [4, 64], P('dom'), may hold values from 0.5 to 8
Outputs:
- mixed: bfloat16 [4, 2048, 4096], P('dom', 'seq')
Inputs may be any that keep to these rules, and one draw needn't show every extreme that they name: Each row of domain_ids names every domain once.
All inputs are finite; a program needn't handle non-finite values.
Results may differ from a plain program's by a relative error of at most 0.0056.
Values may be sent and summed in bfloat16 or wider, within the bound.
A program may use at most 192 MiB of HBM per device.

v0:
```python
import jax
import jax.numpy as jnp
from jax import lax
from jax.sharding import PartitionSpec as P

SPAN = 256


def shifted(block, axis, distance):
    devices = range(lax.axis_size(axis))
    route = [(i - distance, i) for i in devices if i - distance in devices]
    return lax.ppermute(block, axis, route)


def per_device(
    tokens_x, gate_z, in_b, in_c, log_decay, domain_ids, out_weight, norm_gain, skip_gain
):
    groups = lax.axis_size("dom")
    rows = tokens_x.shape[0]
    seg_rows = rows // groups
    order = jnp.argsort(domain_ids.reshape(groups))

    def arrange(value_rows):
        return jnp.take(value_rows.reshape(groups, seg_rows, value_rows.shape[-1]), order, axis=0)

    received = (
        lax.all_to_all(arrange(tokens_x), "dom", split_axis=0, concat_axis=0, tiled=True),
        lax.all_to_all(arrange(gate_z), "dom", split_axis=0, concat_axis=0, tiled=True),
        lax.all_to_all(arrange(in_b), "dom", split_axis=0, concat_axis=0, tiled=True),
        lax.all_to_all(arrange(in_c), "dom", split_axis=0, concat_axis=0, tiled=True),
        lax.all_to_all(arrange(log_decay), "dom", split_axis=0, concat_axis=0, tiled=True),
    )
    xs, zs, bs, cs, ls = [piece.reshape(rows, piece.shape[-1]) for piece in received]
    heads = skip_gain.shape[-1]
    width = xs.shape[1]
    hsize = width // heads
    nstate = bs.shape[1]
    blocks = rows // SPAN
    xc = xs.reshape(blocks, SPAN, heads, hsize)
    bc = bs.reshape(blocks, SPAN, nstate)
    cc = cs.reshape(blocks, SPAN, nstate)
    cum = jnp.cumsum(ls.astype(jnp.float32).reshape(blocks, SPAN, heads), axis=1)
    scores = jnp.einsum("cin,cjn->cij", cc, bc, preferred_element_type=jnp.float32)
    cum_heads = jnp.transpose(cum, (0, 2, 1))
    diff = cum_heads[:, :, :, None] - cum_heads[:, :, None, :]
    positions = jnp.arange(SPAN)
    lower = positions[:, None] >= positions[None, :]
    decay = jnp.where(lower[None, None], jnp.exp(jnp.minimum(diff, 0.0)), 0.0)
    weights = (scores[:, None] * decay).astype(jnp.bfloat16)
    inner = jnp.einsum("chij,cjhp->cihp", weights, xc, preferred_element_type=jnp.float32)
    totals = cum[:, -1, :]
    decayed = (xc.astype(jnp.float32) * jnp.exp(totals[:, None, :] - cum)[..., None]).astype(
        jnp.bfloat16
    )
    block_state = jnp.einsum("cjhp,cjn->chpn", decayed, bc, preferred_element_type=jnp.float32)
    running = jnp.zeros((heads, hsize, nstate), jnp.float32)
    before = [running]
    running = jnp.exp(totals[0])[:, None, None] * running + block_state[0]
    local_end = running
    local_before = jnp.stack(before, axis=0)
    shard_decay = jnp.exp(jnp.sum(totals, axis=0))
    empty_state = jnp.zeros((heads, hsize, nstate), jnp.float32)

    def hop(step, incoming):
        return shifted(shard_decay[:, None, None] * incoming + local_end, "seq", 1)

    incoming = lax.fori_loop(0, lax.axis_size("seq") - 1, hop, empty_state)
    prefix = jnp.cumsum(totals, axis=0) - totals
    full_before = local_before + jnp.exp(prefix)[:, :, None, None] * incoming[None]
    carried = jnp.einsum(
        "cin,chpn->cihp", cc.astype(jnp.float32), full_before, precision=lax.Precision.HIGHEST
    )
    ys = (
        inner
        + jnp.exp(cum)[..., None] * carried
        + skip_gain[0][None, None, :, None] * xc.astype(jnp.float32)
    )
    gated = ys.reshape(rows, width) * jax.nn.silu(zs.astype(jnp.float32))
    normed = (
        gated
        * lax.rsqrt(jnp.mean(gated * gated, axis=-1, keepdims=True) + 1e-05)
        * norm_gain[0][None, :]
    ).astype(jnp.bfloat16)
    mixed = jnp.dot(
        normed,
        lax.all_gather(out_weight[0], "seq", axis=1, tiled=True),
        preferred_element_type=jnp.float32,
    ).astype(jnp.bfloat16)
    return mixed.reshape(1, rows, mixed.shape[-1])


def solution(mesh):
    in_specs = (
        P(("dom", "seq"), None),
        P(("dom", "seq"), None),
        P(("dom", "seq"), None),
        P(("dom", "seq"), None),
        P(("dom", "seq"), None),
        P("dom", "seq", None),
        P("dom", None, "seq"),
        P("dom", None),
        P("dom", None),
    )
    out_specs = P("dom", "seq", None)
    return jax.shard_map(
        per_device, mesh=mesh, in_specs=in_specs, out_specs=out_specs, check_vma=False
    )
```

profile of v0, /device:TPU:0, one launch (start us, length us, event | category | flops | bytes accessed | tf_op | source)
XLA Modules:
  0.0 1014.1 jit_solution(17725002716120116084)
XLA Ops:
  6.6 0.7 all-gather.3.cloned.1.call-update
  7.3 0.2 copy-done.6
  7.4 0.1 copy.25
  7.6 0.7 sort.17
  8.3 0.6 gather_fusion
  9.0 0.7 reshape.348
  9.7 4.2 all-to-all-start.3
  14.0 0.6 gather_fusion.2
  14.6 0.6 gather_fusion.3
  15.1 0.7 broadcast_select_fusion.2
  15.9 2.1 all-to-all-done.3
  17.9 3.3 all-to-all-start.2
  21.2 2.0 gather_fusion.1
  23.2 3.7 gather_fusion.4
  27.0 3.3 all-to-all-start.1
  30.3 4.1 broadcast_select_fusion
  34.4 3.6 all-to-all-start
  38.3 0.6 reduce-window.6
  38.9 0.2 slice_reduce_fusion
  39.2 0.1 broadcast.133
  39.4 0.1 fusion.31
  39.5 0.9 slice_reduce_fusion.1
  40.4 0.2 subtract_exponential_fusion
  40.6 23.0 %all-to-all-done = bf16[4,64,4096]{2,1,0:T(8,128)(2,1)S(1)} async-done(((bf16[4,64,4096]{2,1,0:T(8,128)(2,1)}), bf16[4,64,4096]{2,1,0:T(8,128)(2,1)S(1)}, u32[]{:S(2)}, u32[]{:S(2)}) %all-to-all-start) | async-done | bytes 2097184 | tf_op jit(solution)/shard_map/all_to_all | solution.py:27
  63.6 4.5 all-to-all-start.4
  68.3 4.6 mul.133
  72.9 7.9 mul.134
  80.8 0.2 fusion.32
  81.0 4.2 multiply_convert_fusion.2
  85.2 6.9 convert_element_type.75
  92.1 5.5 reshape.286
  97.7 7.8 copy.34
  105.4 7.0 reshape.288
  112.4 7.8 copy.37
  120.2 5.6 reshape.269
  125.8 7.1 fusion.26
  132.9 14.2 %fusion.2 = f32[64,64,256]{2,1,0:T(8,128)} fusion(f32[64,256]{1,0:T(8,128)S(1)} %bitcast_add_fusion.1, f32[256,256]{1,0:T(8,128)S(1)} %fusion.32, pred[256,256]{1,0:T(8,128)(4,1)S(1)} %iota_compare_fusion, bf16[256,64,64]{2,1,0:T(8,128)(2,1)S(1)} %copy-done.3), kind=kOutput, calls=%fused_computation.9 | convolution fusion | flops 557842432 | bytes 6684672 | tf_op jit(solution)/shard_map/chij,cjhp->cihp/dot_general | solution.py:50
  147.1 1.6 broadcast.134
  148.7 820.7 %while.10 = (s32[]{:T(128)}, f32[64,64,128]{2,1,0:T(8,128)}, f32[64]{0:T(128)S(1)}, f32[64,64,128]{2,1,0:T(8,128)S(1)}, s32[]{:T(128)}) while((s32[]{:T(128)}, f32[64,64,128]{2,1,0:T(8,128)}, f32[64]{0:T(128)S(1)}, f32[64,64,128]{2,1,0:T(8,128)S(1)}, s32[]{:T(128)}) %tuple.26), condition=%wide.region_4.7_spmd, body=%wide.region_3.6_spmd.sunk | while | flops 1048578 | bytes 14680421 | solution.py:67
  148.7 3.2 multiply_add_fusion.2
  151.9 5.0 collective-permute-start
  157.0 89.7 %collective-permute-done = f32[64,64,128]{2,1,0:T(8,128)} collective-permute-done((f32[64,64,128]{2,1,0:T(8,128)}, f32[64,64,128]{2,1,0:T(8,128)}, u32[]{:S(2)}, u32[]{:S(2)}) %collective-permute-start) | collective-permute-done | bytes 2097184 | tf_op jit(solution)/shard_map/while/body/eval_jaxpr/ppermute | solution.py:12
  246.7 3.2 multiply_add_fusion.2
  249.9 5.7 collective-permute-start
  255.6 134.4 %collective-permute-done = f32[64,64,128]{2,1,0:T(8,128)} collective-permute-done((f32[64,64,128]{2,1,0:T(8,128)}, f32[64,64,128]{2,1,0:T(8,128)}, u32[]{:S(2)}, u32[]{:S(2)}) %collective-permute-start) | collective-permute-done | bytes 2097184 | tf_op jit(solution)/shard_map/while/body/eval_jaxpr/ppermute | solution.py:12
  390.0 3.2 multiply_add_fusion.2
  393.1 5.7 collective-permute-start
  398.8 117.2 %collective-permute-done = f32[64,64,128]{2,1,0:T(8,128)} collective-permute-done((f32[64,64,128]{2,1,0:T(8,128)}, f32[64,64,128]{2,1,0:T(8,128)}, u32[]{:S(2)}, u32[]{:S(2)}) %collective-permute-start) | collective-permute-done | bytes 2097184 | tf_op jit(solution)/shard_map/while/body/eval_jaxpr/ppermute | solution.py:12
  516.1 3.2 multiply_add_fusion.2
  519.2 5.5 collective-permute-start
  524.8 126.1 %collective-permute-done = f32[64,64,128]{2,1,0:T(8,128)} collective-permute-done((f32[64,64,128]{2,1,0:T(8,128)}, f32[64,64,128]{2,1,0:T(8,128)}, u32[]{:S(2)}, u32[]{:S(2)}) %collective-permute-start) | collective-permute-done | bytes 2097184 | tf_op jit(solution)/shard_map/while/body/eval_jaxpr/ppermute | solution.py:12
  650.9 3.2 multiply_add_fusion.2
  654.1 5.5 collective-permute-start
  659.6 126.1 %collective-permute-done = f32[64,64,128]{2,1,0:T(8,128)} collective-permute-done((f32[64,64,128]{2,1,0:T(8,128)}, f32[64,64,128]{2,1,0:T(8,128)}, u32[]{:S(2)}, u32[]{:S(2)}) %collective-permute-start) | collective-permute-done | bytes 2097184 | tf_op jit(solution)/shard_map/while/body/eval_jaxpr/ppermute | solution.py:12
  785.7 3.2 multiply_add_fusion.2
  788.9 5.5 collective-permute-start
  794.4 121.9 %collective-permute-done = f32[64,64,128]{2,1,0:T(8,128)} collective-permute-done((f32[64,64,128]{2,1,0:T(8,128)}, f32[64,64,128]{2,1,0:T(8,128)}, u32[]{:S(2)}, u32[]{:S(2)}) %collective-permute-start) | collective-permute-done | bytes 2097184 | tf_op jit(solution)/shard_map/while/body/eval_jaxpr/ppermute | solution.py:12
  916.4 3.2 multiply_add_fusion.2
  919.5 5.7 collective-permute-start
  925.2 44.2 %collective-permute-done = f32[64,64,128]{2,1,0:T(8,128)} collective-permute-done((f32[64,64,128]{2,1,0:T(8,128)}, f32[64,64,128]{2,1,0:T(8,128)}, u32[]{:S(2)}, u32[]{:S(2)}) %collective-permute-start) | collective-permute-done | bytes 2097184 | tf_op jit(solution)/shard_map/while/body/eval_jaxpr/ppermute | solution.py:12
  969.4 9.6 multiply_reduce_fusion
  979.0 5.6 copy.35
  984.6 5.8 fusion.24
  990.5 16.8 %fusion.11 = bf16[1,256,4096]{2,1,0:T(8,128)(2,1)} fusion(bf16[256,4096]{1,0:T(8,128)(2,1)} %fusion.24, bf16[1,4096,4096]{2,1,0:T(8,128)(2,1)} %all-gather.3.cloned.1.call-done), kind=kOutput, calls=%fused_computation.16 | convolution fusion | flops 8590983168 | bytes 37748736 | tf_op jit(solution)/shard_map/dot_general | solution.py:84
  (44 shorter events, 0.8 us)
Async XLA Ops:
  6.5 14.7 %copy-start = (bf16[256,4096]{1,0:T(8,128)(2,1)S(1)}, bf16[256,4096]{1,0:T(8,128)(2,1)}, u32[]{:S(2)}) copy-start(bf16[256,4096]{1,0:T(8,128)(2,1)} %param.15) | copy-start | bytes 6291460
  6.5 0.9 copy-start.6
  6.5 1.0 copy-start.8
  6.5 7.4 copy-start.4
  6.5 8.0 copy-start.5
  6.5 983.9 %all-gather.3.cloned.1.call-start = ((), (), s32[]{:S(2)}) async-start(), calls=%async_computation.5 | async-start | bytes 37748736 | tf_op jit(solution)/shard_map/all_gather | solution.py:86
  9.7 8.2 all-to-all-start.3
  17.9 9.1 all-to-all-start.2
  23.2 7.0 copy-start.2
  27.0 7.4 all-to-all-start.1
  34.4 29.3 %all-to-all-start = ((bf16[4,64,4096]{2,1,0:T(8,128)(2,1)}), bf16[4,64,4096]{2,1,0:T(8,128)(2,1)S(1)}, u32[]{:S(2)}, u32[]{:S(2)}) async-start(bf16[4,64,4096]{2,1,0:T(8,128)(2,1)} %get-tuple-element.43), calls=%async_computation | async-start | bytes 4194304 | tf_op jit(solution)/shard_map/all_to_all | solution.py:27
  63.6 41.8 %all-to-all-start.4 = ((bf16[4,64,4096]{2,1,0:T(8,128)(2,1)}), bf16[4,64,4096]{2,1,0:T(8,128)(2,1)}, u32[]{:S(2)}, u32[]{:S(2)}) async-start(bf16[4,64,4096]{2,1,0:T(8,128)(2,1)} %get-tuple-element.42), calls=%async_computation.4 | async-start | bytes 4194304 | tf_op jit(solution)/shard_map/all_to_all | solution.py:28
  125.8 7.2 copy-start.3
  148.7 820.7 %copy-start.9 = (f32[1,64]{1,0:T(1,128)S(1)}, f32[1,64]{1,0:T(1,128)}, u32[]{:S(2)}) copy-start(f32[1,64]{1,0:T(1,128)} %param.23) | copy-start | bytes 772
  151.9 94.8 %collective-permute-start = (f32[64,64,128]{2,1,0:T(8,128)}, f32[64,64,128]{2,1,0:T(8,128)}, u32[]{:S(2)}, u32[]{:S(2)}) collective-permute-start(f32[64,64,128]{2,1,0:T(8,128)} %multiply_add_fusion.2), channel_id=1, source_target_pairs={{0,1},{1,2},{2,3},{3,4},{4,5},{5,6},{6,7},{8,9},{9,10},{10,11},{11... | collective-permute-start | bytes 6291464 | tf_op jit(solution)/shard_map/while/body/eval_jaxpr/ppermute | solution.py:12
  249.9 140.1 %collective-permute-start = (f32[64,64,128]{2,1,0:T(8,128)}, f32[64,64,128]{2,1,0:T(8,128)}, u32[]{:S(2)}, u32[]{:S(2)}) collective-permute-start(f32[64,64,128]{2,1,0:T(8,128)} %multiply_add_fusion.2), channel_id=1, source_target_pairs={{0,1},{1,2},{2,3},{3,4},{4,5},{5,6},{6,7},{8,9},{9,10},{10,11},{11... | collective-permute-start | bytes 6291464 | tf_op jit(solution)/shard_map/while/body/eval_jaxpr/ppermute | solution.py:12
  393.1 122.9 %collective-permute-start = (f32[64,64,128]{2,1,0:T(8,128)}, f32[64,64,128]{2,1,0:T(8,128)}, u32[]{:S(2)}, u32[]{:S(2)}) collective-permute-start(f32[64,64,128]{2,1,0:T(8,128)} %multiply_add_fusion.2), channel_id=1, source_target_pairs={{0,1},{1,2},{2,3},{3,4},{4,5},{5,6},{6,7},{8,9},{9,10},{10,11},{11... | collective-permute-start | bytes 6291464 | tf_op jit(solution)/shard_map/while/body/eval_jaxpr/ppermute | solution.py:12
  519.2 131.6 %collective-permute-start = (f32[64,64,128]{2,1,0:T(8,128)}, f32[64,64,128]{2,1,0:T(8,128)}, u32[]{:S(2)}, u32[]{:S(2)}) collective-permute-start(f32[64,64,128]{2,1,0:T(8,128)} %multiply_add_fusion.2), channel_id=1, source_target_pairs={{0,1},{1,2},{2,3},{3,4},{4,5},{5,6},{6,7},{8,9},{9,10},{10,11},{11... | collective-permute-start | bytes 6291464 | tf_op jit(solution)/shard_map/while/body/eval_jaxpr/ppermute | solution.py:12
  654.1 131.6 %collective-permute-start = (f32[64,64,128]{2,1,0:T(8,128)}, f32[64,64,128]{2,1,0:T(8,128)}, u32[]{:S(2)}, u32[]{:S(2)}) collective-permute-start(f32[64,64,128]{2,1,0:T(8,128)} %multiply_add_fusion.2), channel_id=1, source_target_pairs={{0,1},{1,2},{2,3},{3,4},{4,5},{5,6},{6,7},{8,9},{9,10},{10,11},{11... | collective-permute-start | bytes 6291464 | tf_op jit(solution)/shard_map/while/body/eval_jaxpr/ppermute | solution.py:12
  788.9 127.5 %collective-permute-start = (f32[64,64,128]{2,1,0:T(8,128)}, f32[64,64,128]{2,1,0:T(8,128)}, u32[]{:S(2)}, u32[]{:S(2)}) collective-permute-start(f32[64,64,128]{2,1,0:T(8,128)} %multiply_add_fusion.2), channel_id=1, source_target_pairs={{0,1},{1,2},{2,3},{3,4},{4,5},{5,6},{6,7},{8,9},{9,10},{10,11},{11... | collective-permute-start | bytes 6291464 | tf_op jit(solution)/shard_map/while/body/eval_jaxpr/ppermute | solution.py:12
  919.5 49.8 %collective-permute-start = (f32[64,64,128]{2,1,0:T(8,128)}, f32[64,64,128]{2,1,0:T(8,128)}, u32[]{:S(2)}, u32[]{:S(2)}) collective-permute-start(f32[64,64,128]{2,1,0:T(8,128)} %multiply_add_fusion.2), channel_id=1, source_target_pairs={{0,1},{1,2},{2,3},{3,4},{4,5},{5,6},{6,7},{8,9},{9,10},{10,11},{11... | collective-permute-start | bytes 6291464 | tf_op jit(solution)/shard_map/while/body/eval_jaxpr/ppermute | solution.py:12
  979.0 5.6 copy-start.7
  990.5 16.8 %copy-start.1 = (bf16[256,4096]{1,0:T(8,128)(2,1)S(1)}, bf16[256,4096]{1,0:T(8,128)(2,1)}, u32[]{:S(2)}) copy-start(bf16[256,4096]{1,0:T(8,128)(2,1)} %param.15) | copy-start | bytes 6291460
Sparse Core Ops, SparseCore 0:
  8.9 892.2 all-gather.2
where the time goes:
time: 1020 us; the launch traced here: 1010 us
  waiting for transfers between devices  785 us (77%)
  local copies, waits for them, and re-layouts  70.5 us (7%)
  starting transfers between devices  57.7 us (6%)
  matrix products  47.9 us (5%)
  other arithmetic  38.9 us (4%)
  between operations  13.6 us (1%)
    ppermute x7, waiting for transfers between devices, shifted(): return lax.ppermute(block, axis, route)  760 us
    ppermute x7, starting transfers between devices, shifted(): return lax.ppermute(block, axis, route)  38.7 us
    all_to_all x1, waiting for transfers between devices, per_device(): lax.all_to_all(arrange(tokens_x), 'dom', split_axis=0, concat_axis=0, til...  23 us
    add x7, other arithmetic, hop(): return shifted(shard_decay[:, None, None] * incoming + local_end, 'seq', 1)  22.3 us
  transfers between devices with their start and end apart: 13, of which 9 were waited for; matrix products, arithmetic and copies ran while one was open for 14% of the time, Pallas kernels for 0%

commit v1 on v0

v1 whole, which is shorter than its diff:
```python
import functools

import jax
import jax.numpy as jnp
from jax import lax
from jax.experimental import pallas as pl
from jax.experimental.pallas import tpu as pltpu
from jax.sharding import PartitionSpec as P

BF = jnp.bfloat16
F32 = jnp.float32
PARTNER = 2


def params(**extra):
    return pltpu.CompilerParams(vmem_limit_bytes=48 * 1024 * 1024, **extra)


def exchange(block, axis, bit):
    size = lax.axis_size(axis)
    return lax.ppermute(block, axis, [(i, i ^ bit) for i in range(size)])


def copy_block(order_ref, *refs):
    half = len(refs) // 2
    for src, dst in zip(refs[:half], refs[half:]):
        dst[...] = src[...]


def arrange(order, arrays, groups):
    seg = arrays[0].shape[0] // groups
    return pl.pallas_call(
        copy_block,
        grid_spec=pltpu.PrefetchScalarGridSpec(
            num_scalar_prefetch=1,
            grid=(groups,),
            in_specs=[
                pl.BlockSpec((seg, a.shape[1]), lambda d, o: (o[d], 0)) for a in arrays
            ],
            out_specs=[pl.BlockSpec((seg, a.shape[1]), lambda d, o: (d, 0)) for a in arrays],
        ),
        out_shape=[jax.ShapeDtypeStruct(a.shape, a.dtype) for a in arrays],
        compiler_params=params(),
        name="arrange",
    )(order, *arrays)


def split2(value):
    high = value.astype(BF)
    low = (value - high.astype(F32)).astype(BF)
    return jnp.concatenate([high, low], axis=1)


def spread(heads, lanes, hsize, start):
    row = lax.broadcasted_iota(jnp.int32, (2 * heads, lanes), 0)
    lane = lax.broadcasted_iota(jnp.int32, (2 * heads, lanes), 1) + start
    row = jnp.where(row >= heads, row - heads, row)
    return jnp.where((lane >= row * hsize) & (lane < (row + 1) * hsize), 1.0, 0.0).astype(BF)


def state_kernel(hsize, x_ref, b_ref, l_ref, state_ref, cum_ref, tail, bt):
    rows, heads = l_ref.shape
    lanes = x_ref.shape[1]

    @pl.when(pl.program_id(0) == 0)
    def _():
        t = lax.broadcasted_iota(jnp.int32, (rows, rows), 0)
        u = lax.broadcasted_iota(jnp.int32, (rows, rows), 1)
        lower = jnp.where(t >= u, 1.0, 0.0).astype(BF)
        cum = jnp.dot(lower, l_ref[...], preferred_element_type=F32)
        cum_ref[...] = cum
        tail[...] = split2(jnp.exp(cum[rows - 1 : rows, :] - cum))
        bt[...] = jnp.transpose(b_ref[...].astype(F32)).astype(BF)

    factor = jnp.dot(
        tail[...],
        spread(heads, lanes, hsize, pl.program_id(0) * lanes),
        preferred_element_type=F32,
    )
    decayed = (x_ref[...].astype(F32) * factor).astype(BF)
    state_ref[0] = jnp.dot(bt[...], decayed, preferred_element_type=F32).astype(BF)


def block_states(xs, bs, ls, parts):
    rows, width = xs.shape
    heads, nstate = ls.shape[1], bs.shape[1]
    lanes = width // parts
    return pl.pallas_call(
        functools.partial(state_kernel, width // heads),
        grid=(parts,),
        in_specs=[
            pl.BlockSpec((rows, lanes), lambda j: (0, j)),
            pl.BlockSpec((rows, nstate), lambda j: (0, 0)),
            pl.BlockSpec((rows, heads), lambda j: (0, 0)),
        ],
        out_specs=[
            pl.BlockSpec((1, nstate, lanes), lambda j: (j, 0, 0)),
            pl.BlockSpec((rows, heads), lambda j: (0, 0)),
        ],
        out_shape=[
            jax.ShapeDtypeStruct((parts, nstate, lanes), BF),
            jax.ShapeDtypeStruct((rows, heads), F32),
        ],
        scratch_shapes=[pltpu.VMEM((rows, 2 * heads), BF), pltpu.VMEM((nstate, rows), BF)],
        cost_estimate=pl.CostEstimate(
            flops=2 * rows * width * nstate, bytes_accessed=4 * rows * width, transcendentals=0
        ),
        compiler_params=params(),
        name="block_states",
    )(xs, bs, ls)


def inner_kernel(hsize, x_ref, b_ref, c_ref, cum_ref, cumt_ref, skip_ref, y_ref, scores):
    rows = x_ref.shape[0]
    group = cumt_ref.shape[1]
    half = rows // 2

    @pl.when(pl.program_id(0) == 0)
    def _():
        scores[...] = lax.dot_general(
            c_ref[...], b_ref[...], (((1,), (1,)), ((), ())), preferred_element_type=F32
        )

    lane = lax.broadcasted_iota(jnp.int32, (half, 2 * hsize), 1)

    def product(part, h, x_pair):
        top = part * half
        cols = top + half
        t = lax.broadcasted_iota(jnp.int32, (half, cols), 0) + top
        u = lax.broadcasted_iota(jnp.int32, (half, cols), 1)
        diff = cum_ref[0, top : top + half, h : h + 1] - cumt_ref[0, h : h + 1, :cols]
        decay = jnp.where(t >= u, jnp.exp(jnp.minimum(diff, 0.0)), 0.0)
        weights = (scores[top : top + half, :cols] * decay).astype(BF)
        return jnp.dot(weights, x_pair[:cols], preferred_element_type=F32)

    for pair in range(group // 2):
        at = slice(pair * 2 * hsize, (pair + 1) * 2 * hsize)
        x_pair = x_ref[:, at]
        for part in range(2):
            span = slice(part * half, (part + 1) * half)
            first = product(part, 2 * pair, x_pair)
            second = product(part, 2 * pair + 1, x_pair)
            y_ref[span, at] = (
                jnp.where(lane < hsize, first, second)
                + skip_ref[:, at] * x_pair[span].astype(F32)
            )


def inner_part(xs, bs, cs, cum, skip):
    rows, width = xs.shape
    heads, nstate = cum.shape[1], bs.shape[1]
    steps = heads // 8
    lanes = width // steps
    cum_groups = jnp.transpose(cum.reshape(rows, steps, 8), (1, 0, 2))
    cumt = jnp.transpose(cum_groups, (0, 2, 1))
    return pl.pallas_call(
        functools.partial(inner_kernel, width // heads),
        grid=(steps,),
        in_specs=[
            pl.BlockSpec((rows, lanes), lambda j: (0, j)),
            pl.BlockSpec((rows, nstate), lambda j: (0, 0)),
            pl.BlockSpec((rows, nstate), lambda j: (0, 0)),
            pl.BlockSpec((1, rows, 8), lambda j: (j, 0, 0)),
            pl.BlockSpec((1, 8, rows), lambda j: (j, 0, 0)),
            pl.BlockSpec((1, lanes), lambda j: (0, j)),
        ],
        out_specs=pl.BlockSpec((rows, lanes), lambda j: (0, j)),
        out_shape=jax.ShapeDtypeStruct((rows, width), F32),
        scratch_shapes=[pltpu.VMEM((rows, rows), F32)],
        cost_estimate=pl.CostEstimate(
            flops=16 * rows * rows * width // 4,
            bytes_accessed=40 * rows * width,
            transcendentals=heads * rows * rows,
        ),
        compiler_params=params(),
        name="inner_part",
    )(xs, bs, cs, cum_groups, cumt, skip)


def prefix_kernel(end_ref, total_ref, before_ref):
    parts = end_ref.shape[0]
    running = jnp.zeros(end_ref.shape[1:], F32)
    for s in range(parts):
        before_ref[s] = running.astype(BF)
        if s < parts - 1:
            running = jnp.exp(total_ref[s : s + 1, :]) * running + end_ref[s].astype(F32)


def prefix_states(ends, totals):
    vmem = pl.BlockSpec(memory_space=pltpu.VMEM)
    return pl.pallas_call(
        prefix_kernel,
        in_specs=[vmem, vmem],
        out_specs=vmem,
        out_shape=jax.ShapeDtypeStruct(ends.shape, BF),
        compiler_params=params(),
        name="prefix_states",
    )(ends, totals)


def norm_kernel(hsize, y_ref, z_ref, c_ref, cum_ref, state_ref, gain_ref, out_ref, gated):
    rows, width = y_ref.shape
    heads = cum_ref.shape[1]
    parts, _, lanes = state_ref.shape
    grown = split2(jnp.exp(cum_ref[...]))
    square = jnp.zeros((rows, 1), F32)
    for j in range(parts):
        at = slice(j * lanes, (j + 1) * lanes)
        carried = jnp.dot(c_ref[...], state_ref[j], preferred_element_type=F32)
        factor = jnp.dot(
            grown, spread(heads, lanes, hsize, j * lanes), preferred_element_type=F32
        )
        y = y_ref[:, at] + factor * carried
        z = z_ref[:, at].astype(F32)
        value = y * (z / (1.0 + jnp.exp(-z)))
        gated[:, at] = value
        square = square + jnp.sum(value * value, axis=1, keepdims=True)
    scale = lax.rsqrt(square / width + 1e-05)
    for j in range(parts):
        at = slice(j * lanes, (j + 1) * lanes)
        out_ref[:, at] = (gated[:, at] * scale * gain_ref[:, at]).astype(BF)


def gated_norm(y, zs, cs, cum, state, gain, row_tile):
    rows, width = y.shape
    heads, nstate = cum.shape[1], cs.shape[1]
    return pl.pallas_call(
        functools.partial(norm_kernel, width // heads),
        grid=(rows // row_tile,),
        in_specs=[
            pl.BlockSpec((row_tile, width), lambda i: (i, 0)),
            pl.BlockSpec((row_tile, width), lambda i: (i, 0)),
            pl.BlockSpec((row_tile, nstate), lambda i: (i, 0)),
            pl.BlockSpec((row_tile, heads), lambda i: (i, 0)),
            pl.BlockSpec(state.shape, lambda i: (0, 0, 0)),
            pl.BlockSpec((1, width), lambda i: (0, 0)),
        ],
        out_specs=pl.BlockSpec((row_tile, width), lambda i: (i, 0)),
        out_shape=jax.ShapeDtypeStruct((rows, width), BF),
        scratch_shapes=[pltpu.VMEM((row_tile, width), F32)],
        cost_estimate=pl.CostEstimate(
            flops=2 * rows * width * nstate,
            bytes_accessed=16 * rows * width,
            transcendentals=rows * width,
        ),
        compiler_params=params(),
        name="gated_norm",
    )(y, zs, cs, cum, state, gain)


def per_device(
    tokens_x, gate_z, in_b, in_c, log_decay, domain_ids, out_weight, norm_gain, skip_gain
):
    groups = lax.axis_size("dom")
    seq = lax.axis_size("seq")
    me = lax.axis_index("seq")
    rows, width = tokens_x.shape
    nstate = in_b.shape[1]
    heads = log_decay.shape[1]
    hsize = width // heads
    columns = out_weight.shape[2]

    bits = [1 << i for i in range(seq.bit_length() - 1) if 1 << i != PARTNER]
    bits = bits[1:][::-1] + bits[:1]
    pieces = {0: out_weight[0]}
    for bit in bits:
        pieces.update({k | bit: exchange(piece, "seq", bit) for k, piece in list(pieces.items())})

    ids = domain_ids.reshape(1, groups)
    order = jnp.sum(
        jnp.where(
            ids == jnp.arange(groups, dtype=jnp.int32)[:, None],
            jnp.arange(groups, dtype=jnp.int32)[None, :],
            0,
        ),
        axis=1,
    ).astype(jnp.int32)
    pad = jnp.zeros((rows, 128 - heads), log_decay.dtype) if heads < 128 else log_decay[:, :0]
    small = jnp.concatenate([in_b, in_c, log_decay, pad], axis=1)
    x_out, z_out, small_out = arrange(order, (tokens_x, gate_z, small), groups)
    send = functools.partial(
        lax.all_to_all, axis_name="dom", split_axis=0, concat_axis=0, tiled=True
    )
    small_in = send(small_out)
    xs = send(x_out)
    zs = send(z_out)
    bs = small_in[:, :nstate]
    cs = small_in[:, nstate : 2 * nstate]
    ls = small_in[:, 2 * nstate : 2 * nstate + heads]

    ends, cum = block_states(xs, bs, ls, seq)
    totals = jnp.broadcast_to(cum[-1].reshape(seq, heads // seq, 1), (seq, heads // seq, hsize))
    totals = totals.reshape(seq, 1, width // seq)
    over = functools.partial(
        lax.all_to_all, axis_name="seq", split_axis=0, concat_axis=0, tiled=True
    )
    totals = over(totals).reshape(seq, width // seq)
    before = over(prefix_states(over(ends), totals))

    skip = jnp.repeat(skip_gain, hsize, axis=1)
    y = inner_part(xs, bs, cs, cum, skip)
    normed = gated_norm(y, zs, cs, cum, before, norm_gain, 64)

    theirs = exchange(normed, "seq", PARTNER)

    def project(acts, piece):
        return jnp.dot(acts, piece, preferred_element_type=F32).astype(BF)

    keys = sorted(pieces)
    outward = jnp.concatenate([project(theirs, pieces[k]) for k in keys], axis=1)
    inward = exchange(outward, "seq", PARTNER)
    out = jnp.zeros((rows, seq * columns), BF)
    for i, k in enumerate(keys):
        out = lax.dynamic_update_slice(out, project(normed, pieces[k]), (0, (me ^ k) * columns))
    for i, k in enumerate(keys):
        block = inward[:, i * columns : (i + 1) * columns]
        out = lax.dynamic_update_slice(out, block, (0, (me ^ (k | PARTNER)) * columns))
    return out[None]


def solution(mesh):
    in_specs = (
        P(("dom", "seq"), None),
        P(("dom", "seq"), None),
        P(("dom", "seq"), None),
        P(("dom", "seq"), None),
        P(("dom", "seq"), None),
        P("dom", "seq", None),
        P("dom", None, "seq"),
        P("dom", None),
        P("dom", None),
    )
    return jax.shard_map(
        per_device, mesh=mesh, in_specs=in_specs, out_specs=P("dom", "seq", None), check_vma=False
    )
```

time: 1020 us -> 443 us (0.43)
  waiting for transfers between devices: 785 us -> 337 us
  local copies, waits for them, and re-layouts: 70.5 us -> 11 us
  other arithmetic: 38.9 us -> 1.82 us
  starting transfers between devices: 57.7 us -> 21.8 us
  blocking collectives: 0 us -> 21.5 us
  Pallas kernels: 0 us -> 20.5 us
  matrix products: 47.9 us -> 29 us
  between operations: 13.6 us -> 0.36 us
    ppermute x7 -> x5, waiting for transfers between devices: 760 us -> 172 us  [exchange(): return lax.ppermute(block, axis, [(i, i ^ bit) for i in range(size)])]
    all_to_all x5 -> x4, waiting for transfers between devices: 25.1 us -> 164 us  [the longest x2 114 us: per_device(): before = over(prefix_states(over(ends), totals))]
    convert_element_type x5 -> x0, local copies, waits for them, and re-layouts: 35 us -> none  [the longest x2 14.8 us: per_device(): gated = ys.reshape(rows, width) * jax.nn.silu(zs.astype(jnp.float32))]
    ppermute x7 -> x5, starting transfers between devices: 38.7 us -> 6.65 us  [exchange(): return lax.ppermute(block, axis, [(i, i ^ bit) for i in range(size)])]
    add x7 -> x0, other arithmetic: 22.3 us -> none  [hop(): return shifted(shard_decay[:, None, None] * incoming + local_end, 'seq', 1)]
    all_to_all x0 -> x2, blocking collectives: none -> 21.5 us  [the longest x1 12.2 us: per_device(): totals = over(totals).reshape(seq, width // seq)]
    pallas_call x0 -> x5, Pallas kernels: none -> 20.5 us  [the longest x1 6.85 us: inner_part(): pl.pallas_call(functools.partial(inner_kernel, width // heads), grid=(ste...]
    dot_general x5 -> x8, matrix products: 47.9 us -> 29 us  [project(): return jnp.dot(acts, piece, preferred_element_type=F32).astype(BF)]
  transfers between devices with their start and end apart: 13 -> 9, of which waited for: 9 -> 7; matrix products, arithmetic and copies ran while one was open for 14% -> 6% of each run, Pallas kernels for 0% -> 3%
where the time goes in v1:
time: 443 us
  waiting for transfers between devices  337 us (76%)
  matrix products  29 us (7%)
  starting transfers between devices  21.8 us (5%)
  blocking collectives  21.5 us (5%)
  Pallas kernels  20.5 us (5%)
  local copies, waits for them, and re-layouts  11 us (2%)
    ppermute x5, waiting for transfers between devices, exchange(): return lax.ppermute(block, axis, [(i, i ^ bit) for i in range(size)])  172 us
    all_to_all x2, waiting for transfers between devices, per_device(): before = over(prefix_states(over(ends), totals))  114 us
    dot_general x8, matrix products, project(): return jnp.dot(acts, piece, preferred_element_type=F32).astype(BF)  29 us
    all_to_all x1, waiting for transfers between devices, per_device(): xs = send(x_out)  25.6 us
    all_to_all x1, waiting for transfers between devices, per_device(): zs = send(z_out)  24.5 us
    all_to_all x1, blocking collectives, per_device(): totals = over(totals).reshape(seq, width // seq)  12.2 us
    all_to_all x1, blocking collectives, per_device(): small_in = send(small_out)  9.36 us
  transfers between devices with their start and end apart: 9, of which 7 were waited for; matrix products, arithmetic and copies ran while one was open for 6% of the time, Pallas kernels for 3%

profile of v1, /device:TPU:0, one launch (start us, length us, event | category | flops | bytes accessed | tf_op | source)
XLA Modules:
  0.0 442.6 jit_solution(13157029947794762260)
XLA Ops:
  0.0 0.8 select_reduce_fusion.order_ref
  0.8 0.9 copy.16
  1.7 0.1 pad.7.clone
  1.7 0.9 maximum_maximum_fusion.refs_2_
  2.7 3.5 arrange.1
  6.2 0.0 copy-start.1
  6.2 1.3 copy-done.1
  7.6 0.0 copy-start.2
  7.6 1.3 copy-done.2
  8.9 9.4 %all_to_all.49 = bf16[4,64,384]{2,1,0:T(8,128)(2,1)S(1)} all-to-all(bf16[4,64,384]{2,1,0:T(8,128)(2,1)S(1)} %bitcast.73), channel_id=1, replica_groups=mesh['dom'=4,'seq'=8] {'dom'}, dimensions={0} | all-to-all | bytes 393216 | tf_op jit(solution)/shard_map/all_to_all | solution.py:284
  18.2 3.6 all-to-all-start
  21.9 25.6 %all-to-all-done = bf16[4,64,4096]{2,1,0:T(8,128)(2,1)S(1)} async-done(((bf16[4,64,4096]{2,1,0:T(8,128)(2,1)}), bf16[4,64,4096]{2,1,0:T(8,128)(2,1)S(1)}, u32[]{:S(2)}, u32[]{:S(2)}) %all-to-all-start) | async-done | bytes 2097184 | tf_op jit(solution)/shard_map/all_to_all | solution.py:285
  47.5 3.8 block_states.1
  51.3 0.0 copy-start.3
  51.3 1.0 copy-done.3
  52.3 0.1 broadcast_in_dim.55
  52.4 0.1 broadcast_in_dim.56
  52.5 0.1 reshape.40
  52.6 12.2 %all_to_all.50 = f32[8,1,512]{2,1,0:T(1,128)S(1)} all-to-all(f32[8,1,512]{2,1,0:T(1,128)S(1)} %reshape.40), channel_id=1, replica_groups=mesh['dom'=4,'seq'=8] {'seq'}, dimensions={0} | all-to-all | bytes 32768 | tf_op jit(solution)/shard_map/all_to_all | solution.py:297
  64.7 3.6 all-to-all-start.3
  68.3 2.8 collective-permute-start.1
  71.1 114.0 %all-to-all-done.3.end_ref = bf16[8,128,512]{2,1,0:T(8,128)(2,1)S(1)} async-done(((bf16[8,128,512]{2,1,0:T(8,128)(2,1)}), bf16[8,128,512]{2,1,0:T(8,128)(2,1)S(1)}, u32[]{:S(2)}, u32[]{:S(2)}) %all-to-all-start.3) | async-done | bytes 1048608 | tf_op jit(solution)/shard_map/all_to_all | solution.py:298
  185.1 4.5 %all-to-all-start.2 = ((bf16[4,64,4096]{2,1,0:T(8,128)(2,1)}), bf16[4,64,4096]{2,1,0:T(8,128)(2,1)}, u32[]{:S(2)}, u32[]{:S(2)}) async-start(bf16[4,64,4096]{2,1,0:T(8,128)(2,1)} %bitcast.69), calls=%async_computation.2 | async-start | bytes 4194304 | tf_op jit(solution)/shard_map/all_to_all | solution.py:286
  189.6 0.0 copy-start.7
  189.6 0.3 prefix_states.1
  189.9 0.0 copy-start
  189.9 1.0 copy-done
  190.8 24.5 %all-to-all-done.2 = bf16[4,64,4096]{2,1,0:T(8,128)(2,1)} async-done(((bf16[4,64,4096]{2,1,0:T(8,128)(2,1)}), bf16[4,64,4096]{2,1,0:T(8,128)(2,1)}, u32[]{:S(2)}, u32[]{:S(2)}) %all-to-all-start.2) | async-done | bytes 2097184 | tf_op jit(solution)/shard_map/all_to_all | solution.py:286
  215.3 3.6 all-to-all-start.5
  218.9 1.9 collective-permute-start
  220.8 65.6 %collective-permute-done.1 = bf16[4096,512]{1,0:T(8,128)(2,1)} collective-permute-done((bf16[4096,512]{1,0:T(8,128)(2,1)}, bf16[4096,512]{1,0:T(8,128)(2,1)}, u32[]{:S(2)}, u32[]{:S(2)}) %collective-permute-start.1) | collective-permute-done | bytes 4194336 | tf_op jit(solution)/shard_map/ppermute | solution.py:21
  286.4 0.3 collective-permute-start.2
  286.7 0.0 copy-done.7
  286.7 0.1 broadcast_in_dim.53
  286.7 0.1 broadcast_in_dim.54.skip_ref
  286.8 0.1 copy.17
  286.9 1.3 copy.18.cum_ref
  288.2 0.0 copy-start.4
  288.2 1.2 copy-done.4
  289.5 6.8 %inner_part.1.y_ref = f32[256,4096]{1,0:T(8,128)} custom-call(bf16[256,4096]{1,0:T(8,128)(2,1)S(1)} %bitcast.68, bf16[256,128]{1,0:T(8,128)(2,1)S(1)} %get-tuple-element.16.b_ref, bf16[256,128]{1,0:T(8,128)(2,1)S(1)} %get-tuple-element.15.c_ref, f32[8,256,8]{2,1,0:T(8,128)S(1)} %copy-done.4, f32[8,8,256]{2,1,0:T(8,128)S(1)} %bitcast.72, ...), custom_call_target="tpu_custom_call" | custom-call | flops 1073741824 | bytes 41943040 | tf_op jit(solution)/shard_map/inner_part/pallas_call | solution.py:156
  296.3 0.0 all-to-all-done.5.state_ref
  296.3 0.0 copy-done.5
  296.3 6.1 %gated_norm.1 = bf16[256,4096]{1,0:T(8,128)(2,1)S(1)} custom-call(f32[256,4096]{1,0:T(8,128)} %inner_part.1.y_ref, bf16[256,4096]{1,0:T(8,128)(2,1)} %bitcast.10.z_ref, bf16[256,128]{1,0:T(8,128)(2,1)S(1)} %get-tuple-element.15.c_ref, f32[256,64]{1,0:T(8,128)S(1)} %get-tuple-element.12.cum_ref, bf16[8,128,512]{2,1,0:T(8,128)(2,1)S(1)} %all-to-all-done.5.state_ref, ...), custom_call_target="tpu_custom_call" | custom-call | flops 268435456 | bytes 16777216 | tf_op jit(solution)/shard_map/gated_norm/pallas_call | solution.py:227
  302.4 0.1 collective-permute-start.3
  302.6 0.2 broadcast_in_dim.49
  302.8 0.0 copy-start.8
  302.8 3.6 fusion.1
  306.4 40.7 %collective-permute-done.3 = bf16[256,4096]{1,0:T(8,128)(2,1)} collective-permute-done((bf16[256,4096]{1,0:T(8,128)(2,1)S(1)}, bf16[256,4096]{1,0:T(8,128)(2,1)}, u32[]{:S(2)}, u32[]{:S(2)}) %collective-permute-start.3) | collective-permute-done | bytes 2097184 | tf_op jit(solution)/shard_map/ppermute | solution.py:21
  347.2 0.0 copy-done.8
  347.2 2.9 convolution_convert_fusion.3
  350.1 4.1 convolution_convert_fusion.1
  354.1 0.0 collective-permute-done
  354.1 4.1 convolution_convert_fusion.2
  358.2 54.1 %collective-permute-done.2 = bf16[4096,512]{1,0:T(8,128)(2,1)} collective-permute-done((bf16[4096,512]{1,0:T(8,128)(2,1)}, bf16[4096,512]{1,0:T(8,128)(2,1)}, u32[]{:S(2)}, u32[]{:S(2)}) %collective-permute-start.2) | collective-permute-done | bytes 4194336 | tf_op jit(solution)/shard_map/ppermute | solution.py:21
  412.4 4.1 convolution_convert_fusion
  416.4 0.1 pad_maximum_fusion
  416.6 1.5 collective-permute-start.4
  418.1 3.4 fusion.3
  421.5 3.4 fusion.5
  425.0 3.4 fusion.7
  428.4 12.0 %collective-permute-done.4 = bf16[256,2048]{1,0:T(8,128)(2,1)S(1)} collective-permute-done((bf16[256,2048]{1,0:T(8,128)(2,1)S(1)}, bf16[256,2048]{1,0:T(8,128)(2,1)S(1)}, u32[]{:S(2)}, u32[]{:S(2)}) %collective-permute-start.4) | collective-permute-done | bytes 1048608 | tf_op jit(solution)/shard_map/ppermute | solution.py:21
  440.5 0.0 copy-start.6
  440.5 1.3 copy-done.6
  441.8 0.7 fusion.8
  (9 shorter events, 0.1 us)
Async XLA Ops:
  6.2 1.4 copy-start.1
  7.6 1.3 copy-start.2
  18.2 29.3 %all-to-all-start = ((bf16[4,64,4096]{2,1,0:T(8,128)(2,1)}), bf16[4,64,4096]{2,1,0:T(8,128)(2,1)S(1)}, u32[]{:S(2)}, u32[]{:S(2)}) async-start(bf16[4,64,4096]{2,1,0:T(8,128)(2,1)} %bitcast.70), calls=%async_computation | async-start | bytes 4194304 | tf_op jit(solution)/shard_map/all_to_all | solution.py:285
  51.3 1.0 copy-start.3
  64.7 120.4 %all-to-all-start.3 = ((bf16[8,128,512]{2,1,0:T(8,128)(2,1)}), bf16[8,128,512]{2,1,0:T(8,128)(2,1)S(1)}, u32[]{:S(2)}, u32[]{:S(2)}) async-start(bf16[8,128,512]{2,1,0:T(8,128)(2,1)} %copy-done.3), calls=%async_computation.3 | async-start | bytes 2097152 | tf_op jit(solution)/shard_map/all_to_all | solution.py:298
  68.3 218.1 %collective-permute-start.1 = (bf16[4096,512]{1,0:T(8,128)(2,1)}, bf16[4096,512]{1,0:T(8,128)(2,1)}, u32[]{:S(2)}, u32[]{:S(2)}) collective-permute-start(bf16[4096,512]{1,0:T(8,128)(2,1)} %bitcast.78), channel_id=1, source_target_pairs={{0,4},{1,5},{2,6},{3,7},{4,0},{5,1},{6,2},{7,3},{8,12},{9,13},{10,... | collective-permute-start | bytes 12582920 | tf_op jit(solution)/shard_map/ppermute | solution.py:21
  185.1 30.2 %all-to-all-start.2 = ((bf16[4,64,4096]{2,1,0:T(8,128)(2,1)}), bf16[4,64,4096]{2,1,0:T(8,128)(2,1)}, u32[]{:S(2)}, u32[]{:S(2)}) async-start(bf16[4,64,4096]{2,1,0:T(8,128)(2,1)} %bitcast.69), calls=%async_computation.2 | async-start | bytes 4194304 | tf_op jit(solution)/shard_map/all_to_all | solution.py:286
  189.6 97.1 %copy-start.7 = (f32[1,64]{1,0:T(1,128)S(1)}, f32[1,64]{1,0:T(1,128)}, u32[]{:S(2)}) copy-start(f32[1,64]{1,0:T(1,128)} %param.17) | copy-start | bytes 772
  189.9 1.0 copy-start
  215.3 81.0 %all-to-all-start.5 = ((bf16[8,128,512]{2,1,0:T(8,128)(2,1)}), bf16[8,128,512]{2,1,0:T(8,128)(2,1)S(1)}, u32[]{:S(2)}, u32[]{:S(2)}) async-start(bf16[8,128,512]{2,1,0:T(8,128)(2,1)} %copy-done), calls=%async_computation.5 | async-start | bytes 2097152 | tf_op jit(solution)/shard_map/all_to_all | solution.py:298
  218.9 135.2 %collective-permute-start = (bf16[4096,512]{1,0:T(8,128)(2,1)}, bf16[4096,512]{1,0:T(8,128)(2,1)}, u32[]{:S(2)}, u32[]{:S(2)}) collective-permute-start(bf16[4096,512]{1,0:T(8,128)(2,1)} %bitcast.79), channel_id=1, source_target_pairs={{0,1},{1,0},{2,3},{3,2},{4,5},{5,4},{6,7},{7,6},{8,9},{9,8},{10,11... | collective-permute-start | bytes 12582920 | tf_op jit(solution)/shard_map/ppermute | solution.py:21
  286.4 126.0 %collective-permute-start.2 = (bf16[4096,512]{1,0:T(8,128)(2,1)}, bf16[4096,512]{1,0:T(8,128)(2,1)}, u32[]{:S(2)}, u32[]{:S(2)}) collective-permute-start(bf16[4096,512]{1,0:T(8,128)(2,1)} %collective-permute-done.1), channel_id=1, source_target_pairs={{0,1},{1,0},{2,3},{3,2},{4,5},{5,4},{6,7},{7,6},{8,9},{9,8},{10,11... | collective-permute-start | bytes 12582920 | tf_op jit(solution)/shard_map/ppermute | solution.py:21
  288.2 1.2 copy-start.4
  289.5 6.9 %copy-start.5 = (f32[1,4096]{1,0:T(1,128)S(1)}, f32[1,4096]{1,0:T(1,128)}, u32[]{:S(2)}) copy-start(f32[1,4096]{1,0:T(1,128)} %gain_ref.1) | copy-start | bytes 49156
  302.4 44.7 %collective-permute-start.3 = (bf16[256,4096]{1,0:T(8,128)(2,1)S(1)}, bf16[256,4096]{1,0:T(8,128)(2,1)}, u32[]{:S(2)}, u32[]{:S(2)}) collective-permute-start(bf16[256,4096]{1,0:T(8,128)(2,1)S(1)} %gated_norm.1), channel_id=1, source_target_pairs={{0,2},{1,3},{2,0},{3,1},{4,6},{5,7},{6,4},{7,5},{8,10},{9,11},{10,... | collective-permute-start | bytes 6291464 | tf_op jit(solution)/shard_map/ppermute | solution.py:21
  302.8 44.3 %copy-start.8 = (bf16[1,4096,512]{2,1,0:T(8,128)(2,1)S(1)}, bf16[1,4096,512]{2,1,0:T(8,128)(2,1)}, u32[]{:S(2)}) copy-start(bf16[1,4096,512]{2,1,0:T(8,128)(2,1)} %param.15) | copy-start | bytes 12582916
  416.6 23.9 %collective-permute-start.4 = (bf16[256,2048]{1,0:T(8,128)(2,1)S(1)}, bf16[256,2048]{1,0:T(8,128)(2,1)S(1)}, u32[]{:S(2)}, u32[]{:S(2)}) collective-permute-start(bf16[256,2048]{1,0:T(8,128)(2,1)S(1)} %pad_maximum_fusion), channel_id=1, source_target_pairs={{0,2},{1,3},{2,0},{3,1},{4,6},{5,7},{6,4},{7,5},{8,10},{9,11},{10,... | collective-permute-start | bytes 3145736 | tf_op jit(solution)/shard_map/ppermute | solution.py:21
  440.5 1.3 copy-start.6

commit v2 on v1

v2 whole, which is shorter than its diff:
```python
import functools

import jax
import jax.numpy as jnp
from jax import lax
from jax.experimental import pallas as pl
from jax.experimental.pallas import tpu as pltpu
from jax.sharding import PartitionSpec as P

BF = jnp.bfloat16
F32 = jnp.float32
PARTNER = 2


def params(**extra):
    return pltpu.CompilerParams(vmem_limit_bytes=48 * 1024 * 1024, **extra)


def exchange(block, axis, bit):
    size = lax.axis_size(axis)
    return lax.ppermute(block, axis, [(i, i ^ bit) for i in range(size)])


def join_block(order_ref, x_ref, z_ref, small_ref, out_ref):
    width = x_ref.shape[1]
    out_ref[:, :width] = x_ref[...]
    out_ref[:, width : 2 * width] = z_ref[...]
    out_ref[:, 2 * width :] = small_ref[...]


def arrange(order, arrays, groups):
    rows = arrays[0].shape[0]
    seg = rows // groups
    total = sum(a.shape[1] for a in arrays)
    return pl.pallas_call(
        join_block,
        grid_spec=pltpu.PrefetchScalarGridSpec(
            num_scalar_prefetch=1,
            grid=(groups,),
            in_specs=[
                pl.BlockSpec((seg, a.shape[1]), lambda d, o: (o[d], 0)) for a in arrays
            ],
            out_specs=pl.BlockSpec((seg, total), lambda d, o: (d, 0)),
        ),
        out_shape=jax.ShapeDtypeStruct((rows, total), BF),
        compiler_params=params(),
        name="arrange",
    )(order, *arrays)


def split2(value):
    high = value.astype(BF)
    low = (value - high.astype(F32)).astype(BF)
    return jnp.concatenate([high, low], axis=1)


def spread(heads, lanes, hsize, start):
    row = lax.broadcasted_iota(jnp.int32, (2 * heads, lanes), 0)
    lane = lax.broadcasted_iota(jnp.int32, (2 * heads, lanes), 1) + start
    row = jnp.where(row >= heads, row - heads, row)
    return jnp.where((lane >= row * hsize) & (lane < (row + 1) * hsize), 1.0, 0.0).astype(BF)


def state_kernel(hsize, heads, x_ref, b_ref, l_ref, state_ref, cum_ref, tail, bt, total):
    rows, lanes = x_ref.shape
    nstate = b_ref.shape[1]

    @pl.when(pl.program_id(0) == 0)
    def _():
        t = lax.broadcasted_iota(jnp.int32, (rows, rows), 0)
        u = lax.broadcasted_iota(jnp.int32, (rows, rows), 1)
        lower = jnp.where(t >= u, 1.0, 0.0).astype(BF)
        cum = jnp.dot(lower, l_ref[:, :heads], preferred_element_type=F32)
        cum_ref[...] = cum
        last = cum[rows - 1 : rows, :]
        tail[...] = split2(jnp.exp(last - cum))
        bt[...] = jnp.transpose(b_ref[...].astype(F32)).astype(BF)
        first = last.astype(BF).astype(F32)
        second = (last - first).astype(BF).astype(F32)
        third = last - first - second
        row = lax.broadcasted_iota(jnp.int32, total.shape, 0)
        total[...] = jnp.where(
            row == 0, first, jnp.where(row == 1, second, jnp.where(row == 2, third, 0.0))
        ).astype(BF)

    choose = spread(heads, lanes, hsize, pl.program_id(0) * lanes)
    factor = jnp.dot(tail[...], choose, preferred_element_type=F32)
    decayed = (x_ref[...].astype(F32) * factor).astype(BF)
    state_ref[0, :nstate] = jnp.dot(bt[...], decayed, preferred_element_type=F32).astype(BF)
    state_ref[0, nstate:] = jnp.dot(
        total[...], choose[:heads], preferred_element_type=F32
    ).astype(BF)


def block_states(joined, width, heads, nstate, parts):
    rows = joined.shape[0]
    lanes = width // parts
    at = 2 * width // nstate
    return pl.pallas_call(
        functools.partial(state_kernel, width // heads, heads),
        grid=(parts,),
        in_specs=[
            pl.BlockSpec((rows, lanes), lambda j: (0, j)),
            pl.BlockSpec((rows, nstate), lambda j: (0, at)),
            pl.BlockSpec((rows, nstate), lambda j: (0, at + 2)),
        ],
        out_specs=[
            pl.BlockSpec((1, nstate + 16, lanes), lambda j: (j, 0, 0)),
            pl.BlockSpec((rows, heads), lambda j: (0, 0)),
        ],
        out_shape=[
            jax.ShapeDtypeStruct((parts, nstate + 16, lanes), BF),
            jax.ShapeDtypeStruct((rows, heads), F32),
        ],
        scratch_shapes=[
            pltpu.VMEM((rows, 2 * heads), BF),
            pltpu.VMEM((nstate, rows), BF),
            pltpu.VMEM((16, heads), BF),
        ],
        cost_estimate=pl.CostEstimate(
            flops=2 * rows * width * nstate, bytes_accessed=4 * rows * width, transcendentals=0
        ),
        compiler_params=params(),
        name="block_states",
    )(joined, joined, joined)


def inner_kernel(hsize, x_ref, b_ref, c_ref, cum_ref, cumt_ref, skip_ref, y_ref, scores):
    rows = x_ref.shape[0]
    group = cumt_ref.shape[1]
    half = rows // 2

    @pl.when(pl.program_id(0) == 0)
    def _():
        scores[...] = lax.dot_general(
            c_ref[...], b_ref[...], (((1,), (1,)), ((), ())), preferred_element_type=F32
        )

    lane = lax.broadcasted_iota(jnp.int32, (half, 2 * hsize), 1)

    def product(part, h, x_pair):
        top = part * half
        cols = top + half
        t = lax.broadcasted_iota(jnp.int32, (half, cols), 0) + top
        u = lax.broadcasted_iota(jnp.int32, (half, cols), 1)
        diff = cum_ref[0, top : top + half, h : h + 1] - cumt_ref[0, h : h + 1, :cols]
        decay = jnp.where(t >= u, jnp.exp(jnp.minimum(diff, 0.0)), 0.0)
        weights = (scores[top : top + half, :cols] * decay).astype(BF)
        return jnp.dot(weights, x_pair[:cols], preferred_element_type=F32)

    for pair in range(group // 2):
        at = slice(pair * 2 * hsize, (pair + 1) * 2 * hsize)
        x_pair = x_ref[:, at]
        for part in range(2):
            span = slice(part * half, (part + 1) * half)
            first = product(part, 2 * pair, x_pair)
            second = product(part, 2 * pair + 1, x_pair)
            y_ref[span, at] = (
                jnp.where(lane < hsize, first, second)
                + skip_ref[:, at] * x_pair[span].astype(F32)
            )


def inner_part(joined, nstate, cum, skip):
    width = skip.shape[1]
    rows, heads = cum.shape
    at = 2 * width // nstate
    steps = heads // 8
    lanes = width // steps
    cum_groups = jnp.transpose(cum.reshape(rows, steps, 8), (1, 0, 2))
    cumt = jnp.transpose(cum_groups, (0, 2, 1))
    return pl.pallas_call(
        functools.partial(inner_kernel, width // heads),
        grid=(steps,),
        in_specs=[
            pl.BlockSpec((rows, lanes), lambda j: (0, j)),
            pl.BlockSpec((rows, nstate), lambda j: (0, at)),
            pl.BlockSpec((rows, nstate), lambda j: (0, at + 1)),
            pl.BlockSpec((1, rows, 8), lambda j: (j, 0, 0)),
            pl.BlockSpec((1, 8, rows), lambda j: (j, 0, 0)),
            pl.BlockSpec((1, lanes), lambda j: (0, j)),
        ],
        out_specs=pl.BlockSpec((rows, lanes), lambda j: (0, j)),
        out_shape=jax.ShapeDtypeStruct((rows, width), F32),
        scratch_shapes=[pltpu.VMEM((rows, rows), F32)],
        cost_estimate=pl.CostEstimate(
            flops=16 * rows * rows * width // 4,
            bytes_accessed=40 * rows * width,
            transcendentals=heads * rows * rows,
        ),
        compiler_params=params(),
        name="inner_part",
    )(joined, joined, joined, cum_groups, cumt, skip)


def prefix_kernel(end_ref, before_ref):
    parts, nstate, _ = before_ref.shape
    running = jnp.zeros(before_ref.shape[1:], F32)
    for s in range(parts):
        before_ref[s] = running.astype(BF)
        if s < parts - 1:
            terms = end_ref[s, nstate:].astype(F32)
            total = jnp.sum(terms, axis=0, keepdims=True)
            running = jnp.exp(total) * running + end_ref[s, :nstate].astype(F32)


def prefix_states(ends):
    parts, tall, lanes = ends.shape
    vmem = pl.BlockSpec(memory_space=pltpu.VMEM)
    return pl.pallas_call(
        prefix_kernel,
        in_specs=[vmem],
        out_specs=vmem,
        out_shape=jax.ShapeDtypeStruct((parts, tall - 16, lanes), BF),
        compiler_params=params(),
        name="prefix_states",
    )(ends)


def norm_kernel(hsize, y_ref, z_ref, c_ref, cum_ref, state_ref, gain_ref, out_ref, gated):
    rows, width = y_ref.shape
    heads = cum_ref.shape[1]
    parts, _, lanes = state_ref.shape
    grown = split2(jnp.exp(cum_ref[...]))
    square = jnp.zeros((rows, 1), F32)
    for j in range(parts):
        at = slice(j * lanes, (j + 1) * lanes)
        carried = jnp.dot(c_ref[...], state_ref[j], preferred_element_type=F32)
        factor = jnp.dot(
            grown, spread(heads, lanes, hsize, j * lanes), preferred_element_type=F32
        )
        y = y_ref[:, at] + factor * carried
        z = z_ref[:, at].astype(F32)
        value = y * (z / (1.0 + jnp.exp(-z)))
        gated[:, at] = value
        square = square + jnp.sum(value * value, axis=1, keepdims=True)
    scale = lax.rsqrt(square / width + 1e-05)
    for j in range(parts):
        at = slice(j * lanes, (j + 1) * lanes)
        out_ref[:, at] = (gated[:, at] * scale * gain_ref[:, at]).astype(BF)


def gated_norm(y, joined, cum, state, gain, row_tile):
    rows, width = y.shape
    heads, nstate = cum.shape[1], state.shape[1]
    at = 2 * width // nstate
    return pl.pallas_call(
        functools.partial(norm_kernel, width // heads),
        grid=(rows // row_tile,),
        in_specs=[
            pl.BlockSpec((row_tile, width), lambda i: (i, 0)),
            pl.BlockSpec((row_tile, width), lambda i: (i, 1)),
            pl.BlockSpec((row_tile, nstate), lambda i: (i, at + 1)),
            pl.BlockSpec((row_tile, heads), lambda i: (i, 0)),
            pl.BlockSpec(state.shape, lambda i: (0, 0, 0)),
            pl.BlockSpec((1, width), lambda i: (0, 0)),
        ],
        out_specs=pl.BlockSpec((row_tile, width), lambda i: (i, 0)),
        out_shape=jax.ShapeDtypeStruct((rows, width), BF),
        scratch_shapes=[pltpu.VMEM((row_tile, width), F32)],
        cost_estimate=pl.CostEstimate(
            flops=2 * rows * width * nstate,
            bytes_accessed=16 * rows * width,
            transcendentals=rows * width,
        ),
        compiler_params=params(),
        name="gated_norm",
    )(y, joined, joined, cum, state, gain)


def per_device(
    tokens_x, gate_z, in_b, in_c, log_decay, domain_ids, out_weight, norm_gain, skip_gain
):
    groups = lax.axis_size("dom")
    seq = lax.axis_size("seq")
    me = lax.axis_index("seq")
    rows, width = tokens_x.shape
    nstate = in_b.shape[1]
    heads = log_decay.shape[1]
    hsize = width // heads
    columns = out_weight.shape[2]

    ids = domain_ids.reshape(1, groups)
    order = jnp.sum(
        jnp.where(
            ids == jnp.arange(groups, dtype=jnp.int32)[:, None],
            jnp.arange(groups, dtype=jnp.int32)[None, :],
            0,
        ),
        axis=1,
    ).astype(jnp.int32)
    pad = jnp.zeros((rows, nstate - heads), log_decay.dtype)
    small = jnp.concatenate([in_b, in_c, log_decay, pad], axis=1)
    joined = lax.all_to_all(
        arrange(order, (tokens_x, gate_z, small), groups),
        "dom",
        split_axis=0,
        concat_axis=0,
        tiled=True,
    )

    unit = columns // 4
    bits = [1 << i for i in range(seq.bit_length() - 1)]
    far = [bit for bit in bits if bit not in (1, PARTNER)]
    own = out_weight[0]

    def cut(first, units):
        return own[:, first * unit : (first + units) * unit]

    def far_pieces(block):
        found = {0: block}
        for bit in far[::-1]:
            found.update({k | bit: exchange(v, "seq", bit) for k, v in list(found.items())})
        del found[0]
        return found

    def forward(found):
        return {k | 1: exchange(v, "seq", 1) for k, v in found.items()}

    done = []

    near_a = exchange(cut(0, 2), "seq", 1)
    far_a = far_pieces(cut(0, 1))
    joined, near_a, far_a = lax.optimization_barrier((joined, near_a, far_a))

    ends, cum = block_states(joined, width, heads, nstate, seq)
    over = functools.partial(
        lax.all_to_all, axis_name="seq", split_axis=0, concat_axis=0, tiled=True
    )
    before = over(prefix_states(over(ends)))
    skip = jnp.repeat(skip_gain, hsize, axis=1)
    y = inner_part(joined, nstate, cum, skip)

    before, far_a, own_b, own_c, own_d = lax.optimization_barrier(
        (before, far_a, cut(1, 2), cut(3, 1), cut(2, 2))
    )
    far_b = far_pieces(own_b)
    near_b = exchange(own_d, "seq", 1)
    forward_a = forward(far_a)
    forward_b = forward(far_b)
    own_c, far_b = lax.optimization_barrier((own_c, far_b))
    far_c = far_pieces(own_c)
    forward_c = forward(far_c)

    normed = gated_norm(y, joined, cum, before, norm_gain, 64)
    theirs = exchange(normed, "seq", PARTNER)
    acts = jnp.concatenate([normed, theirs], axis=0)

    early = [
        (0, {0: own}),
        (0, {1: near_a}),
        (0, far_a),
        (0, forward_a),
        (2, {1: near_b}),
        (1, far_b),
    ]
    late = [(1, forward_b), (3, far_c), (3, forward_c)]

    out = jnp.zeros((rows, seq * columns), BF)
    returned = []
    for batch in (early, late):
        places, blocks = [], []
        for first, found in batch:
            for key, piece in found.items():
                block = jnp.dot(acts, piece, preferred_element_type=F32).astype(BF)
                at = first * unit
                out = lax.dynamic_update_slice(out, block[:rows], (0, (me ^ key) * columns + at))
                places.append((key, at, piece.shape[1]))
                blocks.append(block[rows:])
        returned.append((places, exchange(jnp.concatenate(blocks, axis=1), "seq", PARTNER)))
    for places, block in returned:
        start = 0
        for key, at, wide in places:
            out = lax.dynamic_update_slice(
                out,
                block[:, start : start + wide],
                (0, (me ^ (key | PARTNER)) * columns + at),
            )
            start += wide
    return out[None]


def solution(mesh):
    in_specs = (
        P(("dom", "seq"), None),
        P(("dom", "seq"), None),
        P(("dom", "seq"), None),
        P(("dom", "seq"), None),
        P(("dom", "seq"), None),
        P("dom", "seq", None),
        P("dom", None, "seq"),
        P("dom", None),
        P("dom", None),
    )
    return jax.shard_map(
        per_device, mesh=mesh, in_specs=in_specs, out_specs=P("dom", "seq", None), check_vma=False
    )
```

time: 443 us -> 349 us (0.79)
  waiting for transfers between devices: 337 us -> 201 us
  local copies, waits for them, and re-layouts: 11 us -> 41.1 us
  blocking collectives: 21.5 us -> 33.7 us
  matrix products: 29 us -> 22.3 us
    all_to_all x4 -> x2, waiting for transfers between devices: 164 us -> 15.5 us  [the longest x1 15.5 us: per_device(): before = over(prefix_states(over(ends)))]
    ppermute x5 -> x11, waiting for transfers between devices: 172 us -> 186 us  [exchange(): return lax.ppermute(block, axis, [(i, i ^ bit) for i in range(size)])]
    dynamic_update_slice x4 -> x18, local copies, waits for them, and re-layouts: 0.79 us -> 13.5 us  [the longest x9 7.6 us: per_device(): lax.dynamic_update_slice(out, block[:rows], (0, (me ^ key) * columns + at))]
    all_to_all x2 -> x1, blocking collectives: 21.5 us -> 33.7 us  [per_device(): before = over(prefix_states(over(ends)))]
    broadcast_in_dim x1 -> x24, local copies, waits for them, and re-layouts: 0.23 us -> 8.83 us  [per_device(): return out[None]]
    ppermute x5 -> x11, starting transfers between devices: 6.65 us -> 14.9 us  [exchange(): return lax.ppermute(block, axis, [(i, i ^ bit) for i in range(size)])]
    slice x3 -> x5, local copies, waits for them, and re-layouts: 0.04 us -> 7.89 us  [the longest x2 6.63 us: cut(): return own[:, first * unit:(first + units) * unit]]
    all_to_all x4 -> x2, starting transfers between devices: 15.2 us -> 8.46 us  [the longest x1 4.9 us: per_device(): lax.all_to_all(arrange(order, (tokens_x, gate_z, small), groups), 'dom',...]
  transfers between devices with their start and end apart: 9 -> 13, of which waited for: 7 -> 7; matrix products, arithmetic and copies ran while one was open for 6% -> 15% of each run, Pallas kernels for 3% -> 4%
where the time goes in v2:
time: 349 us
  waiting for transfers between devices  201 us (58%)
  local copies, waits for them, and re-layouts  41.1 us (12%)
  blocking collectives  33.7 us (10%)
  Pallas kernels  24.8 us (7%)
  starting transfers between devices  23.4 us (7%)
  matrix products  22.3 us (6%)
    ppermute x11, waiting for transfers between devices, exchange(): return lax.ppermute(block, axis, [(i, i ^ bit) for i in range(size)])  186 us
    all_to_all x1, blocking collectives, per_device(): before = over(prefix_states(over(ends)))  33.7 us
    dot_general x9, matrix products, per_device(): block = jnp.dot(acts, piece, preferred_element_type=F32).astype(BF)  22.3 us
    all_to_all x1, waiting for transfers between devices, per_device(): before = over(prefix_states(over(ends)))  15.5 us
    ppermute x11, starting transfers between devices, exchange(): return lax.ppermute(block, axis, [(i, i ^ bit) for i in range(size)])  14.9 us
    unnamed x42, local copies, waits for them, and re-layouts  9.51 us
    broadcast_in_dim x24, local copies, waits for them, and re-layouts, per_device(): return out[None]  8.83 us
    dynamic_update_slice x9, local copies, waits for them, and re-layouts, per_device(): lax.dynamic_update_slice(out, block[:rows], (0, (me ^ key) * columns + at))  7.6 us
  transfers between devices with their start and end apart: 13, of which 7 were waited for; matrix products, arithmetic and copies ran while one was open for 15% of the time, Pallas kernels for 4%

profile of v2, /device:TPU:0, one launch (start us, length us, event | category | flops | bytes accessed | tf_op | source)
XLA Modules:
  0.0 348.5 jit_solution(12577255475001665270)
XLA Ops:
  0.0 0.9 copy.31
  0.9 0.8 select_reduce_fusion.order_ref
  1.7 0.9 maximum_maximum_fusion.small_ref
  2.7 1.6 copy-done.1
  4.3 1.6 copy-done.2
  5.8 3.2 arrange.1
  9.0 4.9 %all-to-all-start = ((bf16[4,64,8576]{2,1,0:T(8,128)(2,1)}), bf16[4,64,8576]{2,1,0:T(8,128)(2,1)}, u32[]{:S(2)}, u32[]{:S(2)}) async-start(bf16[4,64,8576]{2,1,0:T(8,128)(2,1)} %bitcast.58), calls=%async_computation | async-start | bytes 8781824 | tf_op jit(solution)/shard_map/all_to_all | solution.py:294
  13.9 5.5 %fusion.1 = (bf16[4096,256]{1,0:T(8,128)(2,1)}, bf16[4096,256]{1,0:T(8,128)(2,1)}, bf16[4096,256]{1,0:T(8,128)(2,1)S(1)}) fusion(bf16[4096,512]{1,0:T(8,128)(2,1)} %bitcast.59), kind=kLoop, calls=%fused_computation.57 | loop fusion | bytes 12582912 | tf_op jit(solution)/shard_map/slice | solution.py:308
  19.4 2.9 collective-permute-start
  22.4 1.1 fusion.2
  23.5 2.6 collective-permute-start.1
  26.1 46.1 %collective-permute-done.1 = bf16[4096,128]{1,0:T(8,128)(2,1)} collective-permute-done((bf16[4096,128]{1,0:T(8,128)(2,1)S(1)}, bf16[4096,128]{1,0:T(8,128)(2,1)}, u32[]{:S(2)}, u32[]{:S(2)}) %collective-permute-start.1) | collective-permute-done | bytes 1048608 | tf_op jit(solution)/shard_map/ppermute | solution.py:21
  72.2 6.3 %block_states.1 = (bf16[8,144,512]{2,1,0:T(8,128)(2,1)S(1)}, f32[256,64]{1,0:T(8,128)S(1)}) custom-call(bf16[256,8576]{1,0:T(8,128)(2,1)} %bitcast.2.x_ref.b_ref.l_ref.c_ref.z_ref, bf16[256,8576]{1,0:T(8,128)(2,1)} %bitcast.2.x_ref.b_ref.l_ref.c_ref.z_ref, bf16[256,8576]{1,0:T(8,128)(2,1)} %bitcast.2.x_ref.b_ref.l_ref.c_ref.z_ref), custom_call_target="tpu_custom_call" | custom-call | flops 268435456 | bytes 4194304 | tf_op jit(solution)/shard_map/block_states/pallas_call | solution.py:99
  78.5 33.7 %all_to_all.22.end_ref = bf16[8,144,512]{2,1,0:T(8,128)(2,1)S(1)} all-to-all(bf16[8,144,512]{2,1,0:T(8,128)(2,1)S(1)} %get-tuple-element.19), channel_id=1, replica_groups=mesh['dom'=4,'seq'=8] {'seq'}, dimensions={0} | all-to-all | bytes 2359296 | tf_op jit(solution)/shard_map/all_to_all | solution.py:330
  112.2 1.3 prefix_states.1
  113.5 3.6 %all-to-all-start.2 = ((bf16[8,128,512]{2,1,0:T(8,128)(2,1)}), bf16[8,128,512]{2,1,0:T(8,128)(2,1)S(1)}, u32[]{:S(2)}, u32[]{:S(2)}) async-start(bf16[8,128,512]{2,1,0:T(8,128)(2,1)} %prefix_states.1), calls=%async_computation.2 | async-start | bytes 2097152 | tf_op jit(solution)/shard_map/all_to_all | solution.py:330
  117.7 7.4 %inner_part.1.y_ref = f32[256,4096]{1,0:T(8,128)S(1)} custom-call(bf16[256,8576]{1,0:T(8,128)(2,1)} %bitcast.2.x_ref.b_ref.l_ref.c_ref.z_ref, bf16[256,8576]{1,0:T(8,128)(2,1)} %bitcast.2.x_ref.b_ref.l_ref.c_ref.z_ref, bf16[256,8576]{1,0:T(8,128)(2,1)} %bitcast.2.x_ref.b_ref.l_ref.c_ref.z_ref, f32[8,256,8]{2,1,0:T(8,128)S(1)} %copy.33.cum_ref, ...), custom_call_target="tpu_custom_call" | custom-call | flops 1073741824 | bytes 41943040 | tf_op jit(solution)/shard_map/inner_part/pallas_call | solution.py:172
  125.1 2.0 copy-done
  127.1 15.5 %all-to-all-done.2.state_ref = bf16[8,128,512]{2,1,0:T(8,128)(2,1)S(1)} async-done(((bf16[8,128,512]{2,1,0:T(8,128)(2,1)}), bf16[8,128,512]{2,1,0:T(8,128)(2,1)S(1)}, u32[]{:S(2)}, u32[]{:S(2)}) %all-to-all-start.2) | async-done | bytes 1048608 | tf_op jit(solution)/shard_map/all_to_all | solution.py:330
  142.6 6.6 %gated_norm.1 = bf16[256,4096]{1,0:T(8,128)(2,1)S(1)} custom-call(f32[256,4096]{1,0:T(8,128)} %copy-done, bf16[256,8576]{1,0:T(8,128)(2,1)} %bitcast.2.x_ref.b_ref.l_ref.c_ref.z_ref, bf16[256,8576]{1,0:T(8,128)(2,1)} %bitcast.2.x_ref.b_ref.l_ref.c_ref.z_ref, f32[256,64]{1,0:T(8,128)S(1)} %get-tuple-element.18.cum_ref, ...), custom_call_target="tpu_custom_call" | custom-call | flops 268435456 | bytes 16777216 | tf_op jit(solution)/shard_map/gated_norm/pallas_call | solution.py:247
  149.2 1.3 collective-permute-start.2
  150.5 1.7 collective-permute-start.3
  152.6 81.6 %collective-permute-done.5 = bf16[4096,256]{1,0:T(8,128)(2,1)S(1)} collective-permute-done((bf16[4096,256]{1,0:T(8,128)(2,1)}, bf16[4096,256]{1,0:T(8,128)(2,1)S(1)}, u32[]{:S(2)}, u32[]{:S(2)}) %collective-permute-start.5) | collective-permute-done | bytes 2097184 | tf_op jit(solution)/shard_map/ppermute | solution.py:21
  234.2 6.4 %collective-permute-done.2 = bf16[256,4096]{1,0:T(8,128)(2,1)S(1)} collective-permute-done((bf16[256,4096]{1,0:T(8,128)(2,1)S(1)}, bf16[256,4096]{1,0:T(8,128)(2,1)S(1)}, u32[]{:S(2)}, u32[]{:S(2)}) %collective-permute-start.2) | collective-permute-done | bytes 2097184 | tf_op jit(solution)/shard_map/ppermute | solution.py:21
  240.6 2.4 convolution_convert_fusion
  243.0 2.9 convolution_convert_fusion.4
  245.9 0.7 slice_dynamic-update-slice_fusion
  246.6 0.7 slice_dynamic-update-slice_fusion.3
  247.3 2.7 convolution_convert_fusion.8
  250.7 1.5 convolution_convert_fusion.7
  252.8 1.3 convolution_convert_fusion.3
  254.1 1.3 convolution_convert_fusion.2
  255.4 0.7 slice_dynamic-update-slice_fusion.2
  256.1 0.7 slice_dynamic-update-slice_fusion.1
  256.9 0.7 copy.37
  257.6 0.7 copy.36
  258.6 2.2 collective-permute-start.6
  260.8 1.6 broadcast_in_dim.62
  262.4 0.7 constant_dynamic-update-slice_fusion.17
  263.1 0.7 constant_dynamic-update-slice_fusion.16
  265.3 0.7 constant_dynamic-update-slice_fusion.13
  265.9 0.7 constant_dynamic-update-slice_fusion.12
  266.6 15.3 %collective-permute-done.7 = bf16[4096,128]{1,0:T(8,128)(2,1)} collective-permute-done((bf16[4096,128]{1,0:T(8,128)(2,1)}, bf16[4096,128]{1,0:T(8,128)(2,1)}, u32[]{:S(2)}, u32[]{:S(2)}) %collective-permute-start.7) | collective-permute-done | bytes 1048608 | tf_op jit(solution)/shard_map/ppermute | solution.py:21
  281.8 2.0 collective-permute-start.8
  283.9 12.9 %collective-permute-done.9 = bf16[256,1536]{0,1:T(8,128)(2,1)S(1)} collective-permute-done((bf16[256,1536]{0,1:T(8,128)(2,1)}, bf16[256,1536]{0,1:T(8,128)(2,1)S(1)}, u32[]{:S(2)}, u32[]{:S(2)}) %collective-permute-start.9) | collective-permute-done | bytes 786464 | tf_op jit(solution)/shard_map/ppermute | solution.py:21
  296.9 0.7 slice_bitcast_fusion.3
  297.7 0.7 copy.45
  298.4 0.7 copy.46
  299.3 1.0 copy.48
  300.3 3.4 convolution_convert_fusion.6
  304.3 0.7 copy.41
  305.0 23.3 %collective-permute-done.8 = bf16[4096,128]{1,0:T(8,128)(2,1)} collective-permute-done((bf16[4096,128]{1,0:T(8,128)(2,1)}, bf16[4096,128]{1,0:T(8,128)(2,1)}, u32[]{:S(2)}, u32[]{:S(2)}) %collective-permute-start.8) | collective-permute-done | bytes 1048608 | tf_op jit(solution)/shard_map/ppermute | solution.py:21
  328.3 3.4 convolution_convert_fusion.5
  332.3 0.7 copy.42
  333.0 3.5 %convolution_convert_fusion.1 = bf16[512,256]{0,1:T(8,128)(2,1)S(1)} fusion(bf16[4096,256]{1,0:T(8,128)(2,1)} %collective-permute-done.6, bf16[256,4096]{1,0:T(8,128)(2,1)} %copy-done.17, bf16[256,4096]{1,0:T(8,128)(2,1)S(1)} %gated_norm.1), kind=kOutput, calls=%fused_computation.2 | convolution fusion | flops 1082261504 | bytes 6553600 | tf_op jit(solution)/shard_map/dot_general | solution.py:365
  336.7 1.8 collective-permute-start.10
  338.6 0.7 constant_dynamic-update-slice_fusion.11
  339.3 1.5 constant_dynamic-update-slice_fusion.10
  340.7 1.5 constant_dynamic-update-slice_fusion.9
  342.2 0.7 constant_dynamic-update-slice_fusion.8
  342.9 0.7 constant_dynamic-update-slice_fusion.7
  344.9 0.7 constant_dynamic-update-slice_fusion.4
  345.5 0.7 constant_dynamic-update-slice_fusion.3
  346.6 0.7 constant_dynamic-update-slice_fusion.2
  (76 shorter events, 8.6 us)
Async XLA Ops:
  2.7 1.6 copy-start.1
  4.3 1.6 copy-start.2
  9.0 63.2 %all-to-all-start = ((bf16[4,64,8576]{2,1,0:T(8,128)(2,1)}), bf16[4,64,8576]{2,1,0:T(8,128)(2,1)}, u32[]{:S(2)}, u32[]{:S(2)}) async-start(bf16[4,64,8576]{2,1,0:T(8,128)(2,1)} %bitcast.58), calls=%async_computation | async-start | bytes 8781824 | tf_op jit(solution)/shard_map/all_to_all | solution.py:294
  13.9 8.5 %copy-start.4 = (bf16[1,4096,512]{2,1,0:T(8,128)(2,1)S(1)}, bf16[1,4096,512]{2,1,0:T(8,128)(2,1)}, u32[]{:S(2)}) copy-start(bf16[1,4096,512]{2,1,0:T(8,128)(2,1)} %param.15) | copy-start | bytes 12582916
  19.4 52.8 %collective-permute-start = (bf16[4096,256]{1,0:T(8,128)(2,1)S(1)}, bf16[4096,256]{1,0:T(8,128)(2,1)}, u32[]{:S(2)}, u32[]{:S(2)}) collective-permute-start(bf16[4096,256]{1,0:T(8,128)(2,1)S(1)} %get-tuple-element.31), channel_id=1, source_target_pairs={{0,1},{1,0},{2,3},{3,2},{4,5},{5,4},{6,7},{7,6},{8,9},{9,8},{10,11... | collective-permute-start | bytes 6291464 | tf_op jit(solution)/shard_map/ppermute | solution.py:21
  23.5 48.7 %collective-permute-start.1 = (bf16[4096,128]{1,0:T(8,128)(2,1)S(1)}, bf16[4096,128]{1,0:T(8,128)(2,1)}, u32[]{:S(2)}, u32[]{:S(2)}) collective-permute-start(bf16[4096,128]{1,0:T(8,128)(2,1)S(1)} %get-tuple-element.33), channel_id=1, source_target_pairs={{0,4},{1,5},{2,6},{3,7},{4,0},{5,1},{6,2},{7,3},{8,12},{9,13},{10,... | collective-permute-start | bytes 3145736 | tf_op jit(solution)/shard_map/ppermute | solution.py:21
  112.2 4.9 %copy-start.15 = (f32[1,64]{1,0:T(1,128)S(1)}, f32[1,64]{1,0:T(1,128)}, u32[]{:S(2)}) copy-start(f32[1,64]{1,0:T(1,128)} %param.17) | copy-start | bytes 772
  113.5 29.1 %all-to-all-start.2 = ((bf16[8,128,512]{2,1,0:T(8,128)(2,1)}), bf16[8,128,512]{2,1,0:T(8,128)(2,1)S(1)}, u32[]{:S(2)}, u32[]{:S(2)}) async-start(bf16[8,128,512]{2,1,0:T(8,128)(2,1)} %prefix_states.1), calls=%async_computation.2 | async-start | bytes 2097152 | tf_op jit(solution)/shard_map/all_to_all | solution.py:330
  117.7 24.9 %copy-start.3 = (f32[1,4096]{1,0:T(1,128)S(1)}, f32[1,4096]{1,0:T(1,128)}, u32[]{:S(2)}) copy-start(f32[1,4096]{1,0:T(1,128)} %gain_ref.1) | copy-start | bytes 49156
  125.1 2.0 copy-start
  142.6 9.7 %copy-start.6 = (bf16[4096,256]{1,0:T(8,128)(2,1)S(1)}, bf16[4096,256]{1,0:T(8,128)(2,1)}, u32[]{:S(2)}) copy-start(bf16[4096,256]{1,0:T(8,128)(2,1)} %get-tuple-element.24) | copy-start | bytes 6291460
  142.6 98.0 %copy-start.5 = (bf16[1,4096,512]{2,1,0:T(8,128)(2,1)S(1)}, bf16[1,4096,512]{2,1,0:T(8,128)(2,1)}, u32[]{:S(2)}) copy-start(bf16[1,4096,512]{2,1,0:T(8,128)(2,1)} %param.15) | copy-start | bytes 12582916
  142.6 91.6 %collective-permute-start.5 = (bf16[4096,256]{1,0:T(8,128)(2,1)}, bf16[4096,256]{1,0:T(8,128)(2,1)S(1)}, u32[]{:S(2)}, u32[]{:S(2)}) collective-permute-start(bf16[4096,256]{1,0:T(8,128)(2,1)} %get-tuple-element.26), channel_id=1, source_target_pairs={{0,4},{1,5},{2,6},{3,7},{4,0},{5,1},{6,2},{7,3},{8,12},{9,13},{10,... | collective-permute-start | bytes 6291464 | tf_op jit(solution)/shard_map/ppermute | solution.py:21
  149.2 91.4 %collective-permute-start.2 = (bf16[256,4096]{1,0:T(8,128)(2,1)S(1)}, bf16[256,4096]{1,0:T(8,128)(2,1)S(1)}, u32[]{:S(2)}, u32[]{:S(2)}) collective-permute-start(bf16[256,4096]{1,0:T(8,128)(2,1)S(1)} %gated_norm.1), channel_id=1, source_target_pairs={{0,2},{1,3},{2,0},{3,1},{4,6},{5,7},{6,4},{7,5},{8,10},{9,11},{10,... | collective-permute-start | bytes 6291464 | tf_op jit(solution)/shard_map/ppermute | solution.py:21
  150.5 100.1 %collective-permute-start.3 = (bf16[4096,128]{1,0:T(8,128)(2,1)}, bf16[4096,128]{1,0:T(8,128)(2,1)S(1)}, u32[]{:S(2)}, u32[]{:S(2)}) collective-permute-start(bf16[4096,128]{1,0:T(8,128)(2,1)} %collective-permute-done.1), channel_id=1, source_target_pairs={{0,1},{1,0},{2,3},{3,2},{4,5},{5,4},{6,7},{7,6},{8,9},{9,8},{10,11... | collective-permute-start | bytes 3145736 | tf_op jit(solution)/shard_map/ppermute | solution.py:21
  152.3 100.5 %collective-permute-start.4 = (bf16[4096,256]{1,0:T(8,128)(2,1)S(1)}, bf16[4096,256]{1,0:T(8,128)(2,1)S(1)}, u32[]{:S(2)}, u32[]{:S(2)}) collective-permute-start(bf16[4096,256]{1,0:T(8,128)(2,1)S(1)} %copy-done.6), channel_id=1, source_target_pairs={{0,1},{1,0},{2,3},{3,2},{4,5},{5,4},{6,7},{7,6},{8,9},{9,8},{10,11... | collective-permute-start | bytes 6291464 | tf_op jit(solution)/shard_map/ppermute | solution.py:21
  234.2 19.9 %copy-start.16 = (bf16[4096,256]{1,0:T(8,128)(2,1)}, bf16[4096,256]{1,0:T(8,128)(2,1)S(1)}, u32[]{:S(2)}) copy-start(bf16[4096,256]{1,0:T(8,128)(2,1)S(1)} %collective-permute-done.5) | copy-start | bytes 6291460
  234.2 47.7 %collective-permute-start.7 = (bf16[4096,128]{1,0:T(8,128)(2,1)}, bf16[4096,128]{1,0:T(8,128)(2,1)}, u32[]{:S(2)}, u32[]{:S(2)}) collective-permute-start(bf16[4096,128]{1,0:T(8,128)(2,1)} %get-tuple-element.28), channel_id=1, source_target_pairs={{0,4},{1,5},{2,6},{3,7},{4,0},{5,1},{6,2},{7,3},{8,12},{9,13},{10,... | collective-permute-start | bytes 3145736 | tf_op jit(solution)/shard_map/ppermute | solution.py:21
  240.6 13.5 %copy-start.17 = (bf16[256,4096]{1,0:T(8,128)(2,1)}, bf16[256,4096]{1,0:T(8,128)(2,1)S(1)}, u32[]{:S(2)}) copy-start(bf16[256,4096]{1,0:T(8,128)(2,1)S(1)} %collective-permute-done.2) | copy-start | bytes 6291460
  256.9 39.9 %collective-permute-start.9 = (bf16[256,1536]{0,1:T(8,128)(2,1)}, bf16[256,1536]{0,1:T(8,128)(2,1)S(1)}, u32[]{:S(2)}, u32[]{:S(2)}) collective-permute-start(bf16[256,1536]{0,1:T(8,128)(2,1)} %get-tuple-element.45), channel_id=1, source_target_pairs={{0,2},{1,3},{2,0},{3,1},{4,6},{5,7},{6,4},{7,5},{8,10},{9,11},{10,... | collective-permute-start | bytes 2359304 | tf_op jit(solution)/shard_map/ppermute | solution.py:21
  258.6 5.2 %copy-start.12 = (bf16[1,256,128]{2,1,0:T(8,128)(2,1)S(1)}, bf16[1,256,128]{2,1,0:T(8,128)(2,1)}, u32[]{:S(2)}) copy-start(bf16[1,256,128]{2,1,0:T(8,128)(2,1)} %copy.36) | copy-start | bytes 196612
  258.6 5.8 %copy-start.11 = (bf16[1,256,128]{2,1,0:T(8,128)(2,1)S(1)}, bf16[1,256,128]{2,1,0:T(8,128)(2,1)}, u32[]{:S(2)}) copy-start(bf16[1,256,128]{2,1,0:T(8,128)(2,1)} %copy.37) | copy-start | bytes 196612
  258.6 6.5 %copy-start.8 = (bf16[1,256,256]{1,2,0:T(8,128)(2,1)S(1)}, bf16[1,256,256]{1,2,0:T(8,128)(2,1)}, u32[]{:S(2)}) copy-start(bf16[1,256,256]{1,2,0:T(8,128)(2,1)} %get-tuple-element.46) | copy-start | bytes 393220
  258.6 6.6 %copy-start.7 = (bf16[1,256,256]{1,2,0:T(8,128)(2,1)S(1)}, bf16[1,256,256]{1,2,0:T(8,128)(2,1)}, u32[]{:S(2)}) copy-start(bf16[1,256,256]{1,2,0:T(8,128)(2,1)} %get-tuple-element.48) | copy-start | bytes 393220
  258.6 74.4 %collective-permute-start.6 = (bf16[4096,256]{1,0:T(8,128)(2,1)}, bf16[4096,256]{1,0:T(8,128)(2,1)}, u32[]{:S(2)}, u32[]{:S(2)}) collective-permute-start(bf16[4096,256]{1,0:T(8,128)(2,1)} %copy-done.16), channel_id=1, source_target_pairs={{0,1},{1,0},{2,3},{3,2},{4,5},{5,4},{6,7},{7,6},{8,9},{9,8},{10,11... | collective-permute-start | bytes 6291464 | tf_op jit(solution)/shard_map/ppermute | solution.py:21
  281.8 46.4 %collective-permute-start.8 = (bf16[4096,128]{1,0:T(8,128)(2,1)}, bf16[4096,128]{1,0:T(8,128)(2,1)}, u32[]{:S(2)}, u32[]{:S(2)}) collective-permute-start(bf16[4096,128]{1,0:T(8,128)(2,1)} %collective-permute-done.7), channel_id=1, source_target_pairs={{0,1},{1,0},{2,3},{3,2},{4,5},{5,4},{6,7},{7,6},{8,9},{9,8},{10,11... | collective-permute-start | bytes 3145736 | tf_op jit(solution)/shard_map/ppermute | solution.py:21
  333.0 3.6 %copy-start.13 = (bf16[256,128]{0,1:T(8,128)(2,1)S(1)}, bf16[256,128]{0,1:T(8,128)(2,1)}, u32[]{:S(2)}) copy-start(bf16[256,128]{0,1:T(8,128)(2,1)} %get-tuple-element.51) | copy-start | bytes 196612
  333.0 3.6 %copy-start.14 = (bf16[256,128]{0,1:T(8,128)(2,1)S(1)}, bf16[256,128]{0,1:T(8,128)(2,1)}, u32[]{:S(2)}) copy-start(bf16[256,128]{0,1:T(8,128)(2,1)} %get-tuple-element.53) | copy-start | bytes 196612
  336.6 7.0 %copy-start.10 = (bf16[1,256,128]{2,1,0:T(8,128)(2,1)S(1)}, bf16[1,256,128]{2,1,0:T(8,128)(2,1)}, u32[]{:S(2)}) copy-start(bf16[1,256,128]{2,1,0:T(8,128)(2,1)} %copy.45) | copy-start | bytes 196612
  336.6 7.6 %copy-start.9 = (bf16[1,256,128]{2,1,0:T(8,128)(2,1)S(1)}, bf16[1,256,128]{2,1,0:T(8,128)(2,1)}, u32[]{:S(2)}) copy-start(bf16[1,256,128]{2,1,0:T(8,128)(2,1)} %copy.46) | copy-start | bytes 196612
  336.7 9.5 %collective-permute-start.10 = (bf16[256,512]{0,1:T(8,128)(2,1)S(1)}, bf16[256,512]{0,1:T(8,128)(2,1)S(1)}, u32[]{:S(2)}, u32[]{:S(2)}) collective-permute-start(bf16[256,512]{0,1:T(8,128)(2,1)S(1)} %pad_maximum_fusion.1), channel_id=1, source_target_pairs={{0,2},{1,3},{2,0},{3,1},{4,6},{5,7},{6,4},{7,5},{8,10},{9,11},{10,... | collective-permute-start | bytes 786440 | tf_op jit(solution)/shard_map/ppermute | solution.py:21

commit v3 on v2

--- a/solution.py
+++ b/solution.py
@@ -9,7 +9,7 @@
 
 BF = jnp.bfloat16
 F32 = jnp.float32
-PARTNER = 2
+PARTNER = 4
 
 
 def params(**extra):
@@ -299,17 +299,13 @@
         tiled=True,
     )
 
-    unit = columns // 4
+    half = columns // 2
     bits = [1 << i for i in range(seq.bit_length() - 1)]
     far = [bit for bit in bits if bit not in (1, PARTNER)]
-    own = out_weight[0]
-
-    def cut(first, units):
-        return own[:, first * unit : (first + units) * unit]
 
     def far_pieces(block):
         found = {0: block}
-        for bit in far[::-1]:
+        for bit in far:
             found.update({k | bit: exchange(v, "seq", bit) for k, v in list(found.items())})
         del found[0]
         return found
@@ -317,66 +313,54 @@
     def forward(found):
         return {k | 1: exchange(v, "seq", 1) for k, v in found.items()}
 
-    done = []
-
-    near_a = exchange(cut(0, 2), "seq", 1)
-    far_a = far_pieces(cut(0, 1))
+    own_a, own_b = out_weight[0, :, :half], out_weight[0, :, half:]
+    far_a = far_pieces(own_a)
+    near_a = exchange(own_a, "seq", 1)
     joined, near_a, far_a = lax.optimization_barrier((joined, near_a, far_a))
+    forward_a = forward(far_a)
 
     ends, cum = block_states(joined, width, heads, nstate, seq)
     over = functools.partial(
         lax.all_to_all, axis_name="seq", split_axis=0, concat_axis=0, tiled=True
     )
-    before = over(prefix_states(over(ends)))
+    prefix = prefix_states(over(ends))
+    prefix, far_own, forward_a = lax.optimization_barrier((prefix, own_b, forward_a))
+    far_b = far_pieces(far_own)
+    before = over(prefix)
     skip = jnp.repeat(skip_gain, hsize, axis=1)
     y = inner_part(joined, nstate, cum, skip)
 
-    before, far_a, own_b, own_c, own_d = lax.optimization_barrier(
-        (before, far_a, cut(1, 2), cut(3, 1), cut(2, 2))
-    )
-    far_b = far_pieces(own_b)
-    near_b = exchange(own_d, "seq", 1)
-    forward_a = forward(far_a)
+    before, near_own = lax.optimization_barrier((before, own_b))
+    near_b = exchange(near_own, "seq", 1)
     forward_b = forward(far_b)
-    own_c, far_b = lax.optimization_barrier((own_c, far_b))
-    far_c = far_pieces(own_c)
-    forward_c = forward(far_c)
 
     normed = gated_norm(y, joined, cum, before, norm_gain, 64)
     theirs = exchange(normed, "seq", PARTNER)
-    acts = jnp.concatenate([normed, theirs], axis=0)
-
-    early = [
-        (0, {0: own}),
-        (0, {1: near_a}),
-        (0, far_a),
-        (0, forward_a),
-        (2, {1: near_b}),
-        (1, far_b),
-    ]
-    late = [(1, forward_b), (3, far_c), (3, forward_c)]
+
+    early = [(0, {0: own_a, 1: near_a}), (half, {0: own_b}), (0, far_a), (0, forward_a)]
+    late = [(half, {1: near_b}), (half, far_b)]
+    last = [(half, forward_b)]
+
+    def project(acts, piece):
+        return jnp.dot(acts, piece, preferred_element_type=F32).astype(BF)
 
     out = jnp.zeros((rows, seq * columns), BF)
     returned = []
-    for batch in (early, late):
+    for batch in (early, late, last):
         places, blocks = [], []
-        for first, found in batch:
+        for at, found in batch:
             for key, piece in found.items():
-                block = jnp.dot(acts, piece, preferred_element_type=F32).astype(BF)
-                at = first * unit
-                out = lax.dynamic_update_slice(out, block[:rows], (0, (me ^ key) * columns + at))
-                places.append((key, at, piece.shape[1]))
-                blocks.append(block[rows:])
-        returned.append((places, exchange(jnp.concatenate(blocks, axis=1), "seq", PARTNER)))
+                out = lax.dynamic_update_slice(
+                    out, project(normed, piece), (0, (me ^ key) * columns + at)
+                )
+                places.append((key, at))
+                blocks.append(project(theirs, piece))
+        returned.append((places, exchange(jnp.stack(blocks), "seq", PARTNER)))
     for places, block in returned:
-        start = 0
-        for key, at, wide in places:
+        for i, (key, at) in enumerate(places):
             out = lax.dynamic_update_slice(
-                out,
-                block[:, start : start + wide],
-                (0, (me ^ (key | PARTNER)) * columns + at),
+                out, block[i], (0, (me ^ (key | PARTNER)) * columns + at)
             )
-            start += wide
     return out[None]
 
 

time: 349 us -> 314 us (0.90)
  waiting for transfers between devices: 201 us -> 160 us
  local copies, waits for them, and re-layouts: 41.1 us -> 14.3 us
  blocking collectives: 33.7 us -> 52.3 us
  matrix products: 22.3 us -> 34.9 us
    ppermute x11 -> x10, waiting for transfers between devices: 186 us -> 147 us  [exchange(): return lax.ppermute(block, axis, [(i, i ^ bit) for i in range(size)])]
    all_to_all x1, blocking collectives: 33.7 us -> 52.3 us  [per_device(): prefix = prefix_states(over(ends))]
    dynamic_update_slice x18 -> x8, local copies, waits for them, and re-layouts: 13.5 us -> 0.77 us  [per_device(): lax.dynamic_update_slice(out, block[i], (0, (me ^ (key | PARTNER)) * colu...]
    dot_general x9 -> x16, matrix products: 22.3 us -> 34.9 us  [project(): return jnp.dot(acts, piece, preferred_element_type=F32).astype(BF)]
    broadcast_in_dim x24 -> x1, local copies, waits for them, and re-layouts: 8.83 us -> 0.23 us  [per_device(): return out[None]]
    slice x5 -> x0, local copies, waits for them, and re-layouts: 7.89 us -> none  [the longest x2 6.63 us: cut(): return own[:, first * unit:(first + units) * unit]]
    squeeze x0 -> x1, local copies, waits for them, and re-layouts: none -> 3.81 us  [per_device(): own_a, own_b = (out_weight[0, :, :half], out_weight[0, :, half:])]
    ppermute x11 -> x10, starting transfers between devices: 14.9 us -> 12.9 us  [exchange(): return lax.ppermute(block, axis, [(i, i ^ bit) for i in range(size)])]
  transfers between devices with their start and end apart: 13 -> 12, of which waited for: 7 -> 7; matrix products, arithmetic and copies ran while one was open for 15% -> 13% of each run, Pallas kernels for 4% -> 7%
where the time goes in v3:
time: 314 us; the launch traced here: 312 us
  waiting for transfers between devices  160 us (51%)
  blocking collectives  52.3 us (17%)
  matrix products  34.9 us (11%)
  Pallas kernels  24.2 us (8%)
  starting transfers between devices  23.7 us (8%)
  local copies, waits for them, and re-layouts  14.3 us (5%)
    ppermute x10, waiting for transfers between devices, exchange(): return lax.ppermute(block, axis, [(i, i ^ bit) for i in range(size)])  147 us
    all_to_all x1, blocking collectives, per_device(): prefix = prefix_states(over(ends))  52.3 us
    dot_general x16, matrix products, project(): return jnp.dot(acts, piece, preferred_element_type=F32).astype(BF)  34.9 us
    all_to_all x1, waiting for transfers between devices, per_device(): before = over(prefix)  13.2 us
    ppermute x10, starting transfers between devices, exchange(): return lax.ppermute(block, axis, [(i, i ^ bit) for i in range(size)])  12.9 us
    unnamed x19, local copies, waits for them, and re-layouts  8.83 us
    pallas_call x1, Pallas kernels, inner_part(): pl.pallas_call(functools.partial(inner_kernel, width // heads), grid=(ste...  7.37 us
    pallas_call x1, Pallas kernels, block_states(): pl.pallas_call(functools.partial(state_kernel, width // heads, heads), gr...  6.3 us
  transfers between devices with their start and end apart: 12, of which 7 were waited for; matrix products, arithmetic and copies ran while one was open for 13% of the time, Pallas kernels for 7%

profile of v3, /device:TPU:0, one launch (start us, length us, event | category | flops | bytes accessed | tf_op | source)
XLA Modules:
  0.0 312.0 jit_solution(17498264565575380979)
XLA Ops:
  0.0 0.9 copy.13
  0.9 0.8 select_reduce_fusion.order_ref
  1.7 0.1 pad.5.clone
  1.7 0.9 maximum_maximum_fusion.small_ref
  2.7 0.0 copy-start.1
  2.7 1.6 copy-done.1
  4.3 1.6 copy-done.2
  5.8 3.0 arrange.1
  8.9 5.0 %all-to-all-start = ((bf16[4,64,8576]{2,1,0:T(8,128)(2,1)}), bf16[4,64,8576]{2,1,0:T(8,128)(2,1)}, u32[]{:S(2)}, u32[]{:S(2)}) async-start(bf16[4,64,8576]{2,1,0:T(8,128)(2,1)} %bitcast.105), calls=%async_computation | async-start | bytes 8781824 | tf_op jit(solution)/shard_map/all_to_all | solution.py:294
  13.9 3.8 %slice_bitcast_fusion = (bf16[4096,256]{1,0:T(8,128)(2,1)}, bf16[4096,256]{1,0:T(8,128)(2,1)S(1)}) fusion(bf16[1,4096,512]{2,1,0:T(8,128)(2,1)} %param.15), kind=kLoop, calls=%fused_computation | loop fusion | bytes 8388608 | tf_op jit(solution)/shard_map/squeeze | solution.py:316
  17.7 2.9 collective-permute-start
  20.6 1.6 collective-permute-start.1
  22.2 44.7 %collective-permute-done = bf16[4096,256]{1,0:T(8,128)(2,1)S(1)} collective-permute-done((bf16[4096,256]{1,0:T(8,128)(2,1)S(1)}, bf16[4096,256]{1,0:T(8,128)(2,1)S(1)}, u32[]{:S(2)}, u32[]{:S(2)}) %collective-permute-start) | collective-permute-done | bytes 2097184 | tf_op jit(solution)/shard_map/ppermute | solution.py:21
  66.9 1.3 copy-done.7
  68.2 0.3 collective-permute-done.1
  68.4 0.0 all-to-all-done
  68.5 1.5 collective-permute-start.2
  69.9 6.3 %block_states.1 = (bf16[8,144,512]{2,1,0:T(8,128)(2,1)S(1)}, f32[256,64]{1,0:T(8,128)S(1)}) custom-call(bf16[256,8576]{1,0:T(8,128)(2,1)} %bitcast.2.x_ref.b_ref.l_ref.c_ref.z_ref, bf16[256,8576]{1,0:T(8,128)(2,1)} %bitcast.2.x_ref.b_ref.l_ref.c_ref.z_ref, bf16[256,8576]{1,0:T(8,128)(2,1)} %bitcast.2.x_ref.b_ref.l_ref.c_ref.z_ref), custom_call_target="tpu_custom_call" | custom-call | flops 268435456 | bytes 4194304 | tf_op jit(solution)/shard_map/block_states/pallas_call | solution.py:99
  76.2 52.3 %all_to_all.22.end_ref = bf16[8,144,512]{2,1,0:T(8,128)(2,1)S(1)} all-to-all(bf16[8,144,512]{2,1,0:T(8,128)(2,1)S(1)} %get-tuple-element.17), channel_id=1, replica_groups=mesh['dom'=4,'seq'=8] {'seq'}, dimensions={0} | all-to-all | bytes 2359296 | tf_op jit(solution)/shard_map/all_to_all | solution.py:326
  128.6 1.3 prefix_states.1
  129.9 5.8 %all-to-all-start.2 = ((bf16[8,128,512]{2,1,0:T(8,128)(2,1)}), bf16[8,128,512]{2,1,0:T(8,128)(2,1)S(1)}, u32[]{:S(2)}, u32[]{:S(2)}) async-start(bf16[8,128,512]{2,1,0:T(8,128)(2,1)} %prefix_states.1), calls=%async_computation.2 | async-start | bytes 2097152 | tf_op jit(solution)/shard_map/all_to_all | solution.py:329
  135.7 0.1 broadcast_in_dim.46
  135.8 0.1 broadcast_in_dim.47.skip_ref
  135.9 0.1 copy.14
  136.0 0.3 copy.15.cum_ref
  136.3 0.0 copy-start.3
  136.3 7.4 %inner_part.1.y_ref = f32[256,4096]{1,0:T(8,128)S(1)} custom-call(bf16[256,8576]{1,0:T(8,128)(2,1)} %bitcast.2.x_ref.b_ref.l_ref.c_ref.z_ref, bf16[256,8576]{1,0:T(8,128)(2,1)} %bitcast.2.x_ref.b_ref.l_ref.c_ref.z_ref, bf16[256,8576]{1,0:T(8,128)(2,1)} %bitcast.2.x_ref.b_ref.l_ref.c_ref.z_ref, f32[8,256,8]{2,1,0:T(8,128)S(1)} %copy.15.cum_ref, ...), custom_call_target="tpu_custom_call" | custom-call | flops 1073741824 | bytes 41943040 | tf_op jit(solution)/shard_map/inner_part/pallas_call | solution.py:172
  143.7 1.9 copy-done
  145.6 2.0 collective-permute-start.4
  147.7 13.2 %all-to-all-done.2.state_ref = bf16[8,128,512]{2,1,0:T(8,128)(2,1)S(1)} async-done(((bf16[8,128,512]{2,1,0:T(8,128)(2,1)}), bf16[8,128,512]{2,1,0:T(8,128)(2,1)S(1)}, u32[]{:S(2)}, u32[]{:S(2)}) %all-to-all-start.2) | async-done | bytes 1048608 | tf_op jit(solution)/shard_map/all_to_all | solution.py:329
  160.9 6.2 %gated_norm.1 = bf16[256,4096]{1,0:T(8,128)(2,1)S(1)} custom-call(f32[256,4096]{1,0:T(8,128)} %copy-done, bf16[256,8576]{1,0:T(8,128)(2,1)} %bitcast.2.x_ref.b_ref.l_ref.c_ref.z_ref, bf16[256,8576]{1,0:T(8,128)(2,1)} %bitcast.2.x_ref.b_ref.l_ref.c_ref.z_ref, f32[256,64]{1,0:T(8,128)S(1)} %get-tuple-element.16.cum_ref, ...), custom_call_target="tpu_custom_call" | custom-call | flops 268435456 | bytes 16777216 | tf_op jit(solution)/shard_map/gated_norm/pallas_call | solution.py:247
  167.1 0.1 collective-permute-start.6
  167.2 1.2 collective-permute-start.3
  168.4 0.2 broadcast_in_dim.42
  168.6 2.5 fusion.1
  171.1 0.0 copy-start.4
  171.1 0.7 fusion.3
  171.8 1.4 copy-done.4
  173.3 0.8 fusion.5
  174.1 2.3 fusion.7
  176.4 2.3 fusion.9
  178.7 53.1 %collective-permute-done.4 = bf16[4096,256]{1,0:T(8,128)(2,1)} collective-permute-done((bf16[4096,256]{1,0:T(8,128)(2,1)}, bf16[4096,256]{1,0:T(8,128)(2,1)}, u32[]{:S(2)}, u32[]{:S(2)}) %collective-permute-start.4) | collective-permute-done | bytes 2097184 | tf_op jit(solution)/shard_map/ppermute | solution.py:21
  231.8 0.5 collective-permute-start.5
  232.3 26.0 %collective-permute-done.6 = bf16[256,4096]{1,0:T(8,128)(2,1)} collective-permute-done((bf16[256,4096]{1,0:T(8,128)(2,1)S(1)}, bf16[256,4096]{1,0:T(8,128)(2,1)}, u32[]{:S(2)}, u32[]{:S(2)}) %collective-permute-start.6) | collective-permute-done | bytes 2097184 | tf_op jit(solution)/shard_map/ppermute | solution.py:21
  258.3 2.9 fusion.27
  261.3 2.9 fusion.26
  264.2 0.1 collective-permute-start.8
  264.3 2.3 fusion.17
  266.7 2.3 fusion.19
  269.0 2.4 fusion.21
  271.4 2.9 fusion.23
  274.3 2.9 fusion.25
  277.2 3.0 collective-permute-start.7
  280.2 2.3 fusion.11
  282.5 2.3 fusion.13
  284.8 0.0 collective-permute-done.5
  284.8 2.3 fusion.28
  287.1 0.1 collective-permute-start.9
  287.2 0.7 fusion.15
  288.0 21.9 %collective-permute-done.7 = bf16[5,256,256]{2,1,0:T(8,128)(2,1)S(1)} collective-permute-done((bf16[5,256,256]{2,1,0:T(8,128)(2,1)S(1)}, bf16[5,256,256]{2,1,0:T(8,128)(2,1)S(1)}, u32[]{:S(2)}, u32[]{:S(2)}) %collective-permute-start.7) | collective-permute-done | bytes 655392 | tf_op jit(solution)/shard_map/ppermute | solution.py:21
  310.0 0.0 copy-start.5
  310.0 1.2 collective-permute-done.9
  311.3 0.1 copy-done.5
  311.4 0.7 constant_dynamic-update-slice_fusion
  (20 shorter events, 0.2 us)
Async XLA Ops:
  2.7 1.6 copy-start.1
  4.3 1.6 copy-start.2
  8.9 59.6 %all-to-all-start = ((bf16[4,64,8576]{2,1,0:T(8,128)(2,1)}), bf16[4,64,8576]{2,1,0:T(8,128)(2,1)}, u32[]{:S(2)}, u32[]{:S(2)}) async-start(bf16[4,64,8576]{2,1,0:T(8,128)(2,1)} %bitcast.105), calls=%async_computation | async-start | bytes 8781824 | tf_op jit(solution)/shard_map/all_to_all | solution.py:294
  17.7 49.2 %collective-permute-start = (bf16[4096,256]{1,0:T(8,128)(2,1)S(1)}, bf16[4096,256]{1,0:T(8,128)(2,1)S(1)}, u32[]{:S(2)}, u32[]{:S(2)}) collective-permute-start(bf16[4096,256]{1,0:T(8,128)(2,1)S(1)} %get-tuple-element.26), channel_id=1, source_target_pairs={{0,1},{1,0},{2,3},{3,2},{4,5},{5,4},{6,7},{7,6},{8,9},{9,8},{10,11... | collective-permute-start | bytes 6291464 | tf_op jit(solution)/shard_map/ppermute | solution.py:21
  20.6 47.8 %collective-permute-start.1 = (bf16[4096,256]{1,0:T(8,128)(2,1)S(1)}, bf16[4096,256]{1,0:T(8,128)(2,1)}, u32[]{:S(2)}, u32[]{:S(2)}) collective-permute-start(bf16[4096,256]{1,0:T(8,128)(2,1)S(1)} %get-tuple-element.26), channel_id=1, source_target_pairs={{0,2},{1,3},{2,0},{3,1},{4,6},{5,7},{6,4},{7,5},{8,10},{9,11},{10,... | collective-permute-start | bytes 6291464 | tf_op jit(solution)/shard_map/ppermute | solution.py:21
  66.9 1.3 copy-start.7
  68.5 61.4 %collective-permute-start.2 = (bf16[4096,256]{1,0:T(8,128)(2,1)}, bf16[4096,256]{1,0:T(8,128)(2,1)}, u32[]{:S(2)}, u32[]{:S(2)}) collective-permute-start(bf16[4096,256]{1,0:T(8,128)(2,1)} %collective-permute-done.1), channel_id=1, source_target_pairs={{0,1},{1,0},{2,3},{3,2},{4,5},{5,4},{6,7},{7,6},{8,9},{9,8},{10,11... | collective-permute-start | bytes 6291464 | tf_op jit(solution)/shard_map/ppermute | solution.py:21
  128.6 7.2 %copy-start.6 = (f32[1,64]{1,0:T(1,128)S(1)}, f32[1,64]{1,0:T(1,128)}, u32[]{:S(2)}) copy-start(f32[1,64]{1,0:T(1,128)} %param.17) | copy-start | bytes 772
  129.9 31.0 %all-to-all-start.2 = ((bf16[8,128,512]{2,1,0:T(8,128)(2,1)}), bf16[8,128,512]{2,1,0:T(8,128)(2,1)S(1)}, u32[]{:S(2)}, u32[]{:S(2)}) async-start(bf16[8,128,512]{2,1,0:T(8,128)(2,1)} %prefix_states.1), calls=%async_computation.2 | async-start | bytes 2097152 | tf_op jit(solution)/shard_map/all_to_all | solution.py:329
  136.3 24.6 %copy-start.3 = (f32[1,4096]{1,0:T(1,128)S(1)}, f32[1,4096]{1,0:T(1,128)}, u32[]{:S(2)}) copy-start(f32[1,4096]{1,0:T(1,128)} %gain_ref.1) | copy-start | bytes 49156
  143.7 1.9 copy-start
  145.6 86.2 %collective-permute-start.4 = (bf16[4096,256]{1,0:T(8,128)(2,1)}, bf16[4096,256]{1,0:T(8,128)(2,1)}, u32[]{:S(2)}, u32[]{:S(2)}) collective-permute-start(bf16[4096,256]{1,0:T(8,128)(2,1)} %get-tuple-element.24), channel_id=1, source_target_pairs={{0,2},{1,3},{2,0},{3,1},{4,6},{5,7},{6,4},{7,5},{8,10},{9,11},{10,... | collective-permute-start | bytes 6291464 | tf_op jit(solution)/shard_map/ppermute | solution.py:21
  167.1 91.2 %collective-permute-start.6 = (bf16[256,4096]{1,0:T(8,128)(2,1)S(1)}, bf16[256,4096]{1,0:T(8,128)(2,1)}, u32[]{:S(2)}, u32[]{:S(2)}) collective-permute-start(bf16[256,4096]{1,0:T(8,128)(2,1)S(1)} %gated_norm.1), channel_id=1, source_target_pairs={{0,4},{1,5},{2,6},{3,7},{4,0},{5,1},{6,2},{7,3},{8,12},{9,13},{10,... | collective-permute-start | bytes 6291464 | tf_op jit(solution)/shard_map/ppermute | solution.py:21
  167.2 94.1 %collective-permute-start.3 = (bf16[4096,256]{1,0:T(8,128)(2,1)}, bf16[4096,256]{1,0:T(8,128)(2,1)}, u32[]{:S(2)}, u32[]{:S(2)}) collective-permute-start(bf16[4096,256]{1,0:T(8,128)(2,1)} %get-tuple-element.24), channel_id=1, source_target_pairs={{0,1},{1,0},{2,3},{3,2},{4,5},{5,4},{6,7},{7,6},{8,9},{9,8},{10,11... | collective-permute-start | bytes 6291464 | tf_op jit(solution)/shard_map/ppermute | solution.py:21
  168.6 2.5 copy-start.8
  171.1 2.2 copy-start.4
  231.8 53.0 %collective-permute-start.5 = (bf16[4096,256]{1,0:T(8,128)(2,1)}, bf16[4096,256]{1,0:T(8,128)(2,1)S(1)}, u32[]{:S(2)}, u32[]{:S(2)}) collective-permute-start(bf16[4096,256]{1,0:T(8,128)(2,1)} %collective-permute-done.4), channel_id=1, source_target_pairs={{0,1},{1,0},{2,3},{3,2},{4,5},{5,4},{6,7},{7,6},{8,9},{9,8},{10,11... | collective-permute-start | bytes 6291464 | tf_op jit(solution)/shard_map/ppermute | solution.py:21
  264.2 45.7 %collective-permute-start.8 = (bf16[2,256,256]{2,1,0:T(8,128)(2,1)S(1)}, bf16[2,256,256]{2,1,0:T(8,128)(2,1)S(1)}, u32[]{:S(2)}, u32[]{:S(2)}) collective-permute-start(bf16[2,256,256]{2,1,0:T(8,128)(2,1)S(1)} %pad_maximum_fusion), channel_id=1, source_target_pairs={{0,4},{1,5},{2,6},{3,7},{4,0},{5,1},{6,2},{7,3},{8,12},{9,13},{10,... | collective-permute-start | bytes 786440 | tf_op jit(solution)/shard_map/ppermute | solution.py:21
  277.2 32.6 %collective-permute-start.7 = (bf16[5,256,256]{2,1,0:T(8,128)(2,1)S(1)}, bf16[5,256,256]{2,1,0:T(8,128)(2,1)S(1)}, u32[]{:S(2)}, u32[]{:S(2)}) collective-permute-start(bf16[5,256,256]{2,1,0:T(8,128)(2,1)S(1)} %fusion.25), channel_id=1, source_target_pairs={{0,4},{1,5},{2,6},{3,7},{4,0},{5,1},{6,2},{7,3},{8,12},{9,13},{10,... | collective-permute-start | bytes 1966088 | tf_op jit(solution)/shard_map/ppermute | solution.py:21
  287.1 24.1 %collective-permute-start.9 = (bf16[1,256,256]{2,1,0:T(8,128)(2,1)S(1)}, bf16[1,256,256]{2,1,0:T(8,128)(2,1)S(1)}, u32[]{:S(2)}, u32[]{:S(2)}) collective-permute-start(bf16[1,256,256]{2,1,0:T(8,128)(2,1)S(1)} %fusion.28), channel_id=1, source_target_pairs={{0,4},{1,5},{2,6},{3,7},{4,0},{5,1},{6,2},{7,3},{8,12},{9,13},{10,... | collective-permute-start | bytes 393224 | tf_op jit(solution)/shard_map/ppermute | solution.py:21
  310.0 1.3 copy-start.5

commit v4 on v3

--- a/solution.py
+++ b/solution.py
@@ -240,18 +240,19 @@
         out_ref[:, at] = (gated[:, at] * scale * gain_ref[:, at]).astype(BF)
 
 
-def gated_norm(y, joined, cum, state, gain, row_tile):
-    rows, width = y.shape
+def gated_norm(y, joined, cum, state, gain, row_tile, start, rows):
+    width = y.shape[1]
+    skip = start // row_tile
     heads, nstate = cum.shape[1], state.shape[1]
     at = 2 * width // nstate
     return pl.pallas_call(
         functools.partial(norm_kernel, width // heads),
         grid=(rows // row_tile,),
         in_specs=[
-            pl.BlockSpec((row_tile, width), lambda i: (i, 0)),
-            pl.BlockSpec((row_tile, width), lambda i: (i, 1)),
-            pl.BlockSpec((row_tile, nstate), lambda i: (i, at + 1)),
-            pl.BlockSpec((row_tile, heads), lambda i: (i, 0)),
+            pl.BlockSpec((row_tile, width), lambda i: (i + skip, 0)),
+            pl.BlockSpec((row_tile, width), lambda i: (i + skip, 1)),
+            pl.BlockSpec((row_tile, nstate), lambda i: (i + skip, at + 1)),
+            pl.BlockSpec((row_tile, heads), lambda i: (i + skip, 0)),
             pl.BlockSpec(state.shape, lambda i: (0, 0, 0)),
             pl.BlockSpec((1, width), lambda i: (0, 0)),
         ],
@@ -324,7 +325,7 @@
         lax.all_to_all, axis_name="seq", split_axis=0, concat_axis=0, tiled=True
     )
     prefix = prefix_states(over(ends))
-    prefix, far_own, forward_a = lax.optimization_barrier((prefix, own_b, forward_a))
+    prefix, far_own = lax.optimization_barrier((prefix, own_b))
     far_b = far_pieces(far_own)
     before = over(prefix)
     skip = jnp.repeat(skip_gain, hsize, axis=1)
@@ -334,32 +335,46 @@
     near_b = exchange(near_own, "seq", 1)
     forward_b = forward(far_b)
 
-    normed = gated_norm(y, joined, cum, before, norm_gain, 64)
-    theirs = exchange(normed, "seq", PARTNER)
-
-    early = [(0, {0: own_a, 1: near_a}), (half, {0: own_b}), (0, far_a), (0, forward_a)]
-    late = [(half, {1: near_b}), (half, far_b)]
+    part = rows // 2
+    first = gated_norm(y, joined, cum, before, norm_gain, 64, 0, part)
+    theirs_first = exchange(first, "seq", PARTNER)
+    second = gated_norm(y, joined, cum, before, norm_gain, 64, part, part)
+    normed = jnp.concatenate([first, second], axis=0)
+    theirs_second = exchange(second, "seq", PARTNER)
+
+    early = [(0, {0: own_a, 1: near_a}), (half, {0: own_b}), (0, far_a)]
+    late = [(0, forward_a), (half, {1: near_b}), (half, far_b)]
     last = [(half, forward_b)]
 
     def project(acts, piece):
         return jnp.dot(acts, piece, preferred_element_type=F32).astype(BF)
 
+    def pieces_of(batch):
+        return [(key, at, piece) for at, found in batch for key, piece in found.items()]
+
     out = jnp.zeros((rows, seq * columns), BF)
+    for key, at, piece in pieces_of(early + late + last):
+        out = lax.dynamic_update_slice(
+            out, project(normed, piece), (0, (me ^ key) * columns + at)
+        )
     returned = []
-    for batch in (early, late, last):
+    for batch, halves in (
+        (early, ((0, theirs_first),)),
+        (early, ((part, theirs_second),)),
+        (late, ((0, theirs_first),)),
+        (late, ((part, theirs_second),)),
+        (last, ((0, theirs_first), (part, theirs_second))),
+    ):
         places, blocks = [], []
-        for at, found in batch:
-            for key, piece in found.items():
-                out = lax.dynamic_update_slice(
-                    out, project(normed, piece), (0, (me ^ key) * columns + at)
-                )
-                places.append((key, at))
-                blocks.append(project(theirs, piece))
+        for key, at, piece in pieces_of(batch):
+            for start, acts in halves:
+                places.append((start, key, at))
+                blocks.append(project(acts, piece))
         returned.append((places, exchange(jnp.stack(blocks), "seq", PARTNER)))
     for places, block in returned:
-        for i, (key, at) in enumerate(places):
+        for i, (start, key, at) in enumerate(places):
             out = lax.dynamic_update_slice(
-                out, block[i], (0, (me ^ (key | PARTNER)) * columns + at)
+                out, block[i], (start, (me ^ (key | PARTNER)) * columns + at)
             )
     return out[None]
 

time: 314 us -> 284 us (0.904)
  blocking collectives: 52.3 us -> 33.2 us
  waiting for transfers between devices: 160 us -> 147 us
  starting transfers between devices: 23.7 us -> 29.2 us
    all_to_all x1, blocking collectives: 52.3 us -> 33.2 us  [per_device(): prefix = prefix_states(over(ends))]
    ppermute x10 -> x13, waiting for transfers between devices: 147 us -> 136 us  [exchange(): return lax.ppermute(block, axis, [(i, i ^ bit) for i in range(size)])]
    ppermute x10 -> x13, starting transfers between devices: 12.9 us -> 20.8 us  [exchange(): return lax.ppermute(block, axis, [(i, i ^ bit) for i in range(size)])]
    dot_general x16 -> x24, matrix products: 34.9 us -> 32.1 us  [project(): return jnp.dot(acts, piece, preferred_element_type=F32).astype(BF)]
    unnamed x19 -> x15, local copies, waits for them, and re-layouts: 8.83 us -> 7.33 us
    pallas_call x1 -> x2, Pallas kernels: 6.2 us -> 7.66 us  [gated_norm(): pl.pallas_call(functools.partial(norm_kernel, width // heads), grid=(rows...]
  transfers between devices with their start and end apart: 12 -> 15, of which waited for: 7 -> 10; matrix products, arithmetic and copies ran while one was open for 13% -> 13% of each run, Pallas kernels for 7% -> 5%
where the time goes in v4:
time: 284 us; the launch traced here: 283 us
  waiting for transfers between devices  147 us (52%)
  blocking collectives  33.2 us (12%)
  matrix products  32.1 us (11%)
  starting transfers between devices  29.2 us (10%)
  Pallas kernels  25.8 us (9%)
  local copies, waits for them, and re-layouts  12.8 us (5%)
    ppermute x13, waiting for transfers between devices, exchange(): return lax.ppermute(block, axis, [(i, i ^ bit) for i in range(size)])  136 us
    all_to_all x1, blocking collectives, per_device(): prefix = prefix_states(over(ends))  33.2 us
    dot_general x24, matrix products, project(): return jnp.dot(acts, piece, preferred_element_type=F32).astype(BF)  32.1 us
    ppermute x13, starting transfers between devices, exchange(): return lax.ppermute(block, axis, [(i, i ^ bit) for i in range(size)])  20.8 us
    all_to_all x1, waiting for transfers between devices, per_device(): before = over(prefix)  11.8 us
    pallas_call x2, Pallas kernels, gated_norm(): pl.pallas_call(functools.partial(norm_kernel, width // heads), grid=(rows...  7.66 us
    pallas_call x1, Pallas kernels, inner_part(): pl.pallas_call(functools.partial(inner_kernel, width // heads), grid=(ste...  7.37 us
    unnamed x15, local copies, waits for them, and re-layouts  7.33 us
  transfers between devices with their start and end apart: 15, of which 10 were waited for; matrix products, arithmetic and copies ran while one was open for 13% of the time, Pallas kernels for 5%

profile of v4, /device:TPU:0, one launch (start us, length us, event | category | flops | bytes accessed | tf_op | source)
XLA Modules:
  0.0 282.9 jit_solution(18043396999626715362)
XLA Ops:
  0.0 0.8 select_reduce_fusion.order_ref
  0.8 0.9 copy.13
  1.7 0.9 maximum_maximum_fusion.small_ref
  2.7 1.6 copy-done.1
  4.3 1.6 copy-done.2
  5.8 3.2 %arrange.1 = bf16[256,8576]{1,0:T(8,128)(2,1)} custom-call(s32[4]{0:T(128)S(1)} %select_reduce_fusion.order_ref, bf16[256,4096]{1,0:T(8,128)(2,1)S(1)} %copy-done.1, bf16[256,4096]{1,0:T(8,128)(2,1)S(1)} %copy-done.2, bf16[256,384]{1,0:T(8,128)(2,1)S(1)} %maximum_maximum_fusion.small_ref), custom_call_target="tpu_custom_call" | custom-call | tf_op jit(solution)/shard_map/arrange/pallas_call | solution.py:35
  9.0 4.9 %all-to-all-start = ((bf16[4,64,8576]{2,1,0:T(8,128)(2,1)}), bf16[4,64,8576]{2,1,0:T(8,128)(2,1)}, u32[]{:S(2)}, u32[]{:S(2)}) async-start(bf16[4,64,8576]{2,1,0:T(8,128)(2,1)} %bitcast.119), calls=%async_computation | async-start | bytes 8781824 | tf_op jit(solution)/shard_map/all_to_all | solution.py:295
  13.9 3.8 %slice_bitcast_fusion = (bf16[4096,256]{1,0:T(8,128)(2,1)}, bf16[4096,256]{1,0:T(8,128)(2,1)S(1)}) fusion(bf16[1,4096,512]{2,1,0:T(8,128)(2,1)} %param.15), kind=kLoop, calls=%fused_computation.1 | loop fusion | bytes 8388608 | tf_op jit(solution)/shard_map/squeeze | solution.py:317
  17.7 2.9 %collective-permute-start = (bf16[4096,256]{1,0:T(8,128)(2,1)S(1)}, bf16[4096,256]{1,0:T(8,128)(2,1)}, u32[]{:S(2)}, u32[]{:S(2)}) collective-permute-start(bf16[4096,256]{1,0:T(8,128)(2,1)S(1)} %get-tuple-element.24), channel_id=1, source_target_pairs={{0,1},{1,0},{2,3},{3,2},{4,5},{5,4},{6,7},{7,6},{8,9},{9,8},{10,11... | collective-permute-start | bytes 6291464 | tf_op jit(solution)/shard_map/ppermute | solution.py:21
  20.7 1.6 collective-permute-start.1
  22.2 44.8 %collective-permute-done = bf16[4096,256]{1,0:T(8,128)(2,1)} collective-permute-done((bf16[4096,256]{1,0:T(8,128)(2,1)S(1)}, bf16[4096,256]{1,0:T(8,128)(2,1)}, u32[]{:S(2)}, u32[]{:S(2)}) %collective-permute-start) | collective-permute-done | bytes 2097184 | tf_op jit(solution)/shard_map/ppermute | solution.py:21
  67.0 1.5 collective-permute-done.1
  68.5 6.3 %block_states.1 = (bf16[8,144,512]{2,1,0:T(8,128)(2,1)S(1)}, f32[256,64]{1,0:T(8,128)S(1)}) custom-call(bf16[256,8576]{1,0:T(8,128)(2,1)} %bitcast.2.x_ref.b_ref.l_ref.c_ref.z_ref, bf16[256,8576]{1,0:T(8,128)(2,1)} %bitcast.2.x_ref.b_ref.l_ref.c_ref.z_ref, bf16[256,8576]{1,0:T(8,128)(2,1)} %bitcast.2.x_ref.b_ref.l_ref.c_ref.z_ref), custom_call_target="tpu_custom_call" | custom-call | flops 268435456 | bytes 4194304 | tf_op jit(solution)/shard_map/block_states/pallas_call | solution.py:99
  74.8 33.2 %all_to_all.22.end_ref = bf16[8,144,512]{2,1,0:T(8,128)(2,1)S(1)} all-to-all(bf16[8,144,512]{2,1,0:T(8,128)(2,1)S(1)} %get-tuple-element.16), channel_id=1, replica_groups=mesh['dom'=4,'seq'=8] {'seq'}, dimensions={0} | all-to-all | bytes 2359296 | tf_op jit(solution)/shard_map/all_to_all | solution.py:327
  108.0 1.3 prefix_states.1
  109.3 3.6 %all-to-all-start.2 = ((bf16[8,128,512]{2,1,0:T(8,128)(2,1)}), bf16[8,128,512]{2,1,0:T(8,128)(2,1)S(1)}, u32[]{:S(2)}, u32[]{:S(2)}) async-start(bf16[8,128,512]{2,1,0:T(8,128)(2,1)} %prefix_states.1), calls=%async_computation.2 | async-start | bytes 2097152 | tf_op jit(solution)/shard_map/all_to_all | solution.py:330
  112.9 1.9 collective-permute-start.2
  114.8 1.5 collective-permute-start.4
  116.3 0.1 broadcast_in_dim.47.skip_ref
  116.6 0.3 copy.15.cum_ref
  117.0 7.4 %inner_part.1.y_ref = f32[256,4096]{1,0:T(8,128)S(1)} custom-call(bf16[256,8576]{1,0:T(8,128)(2,1)} %bitcast.2.x_ref.b_ref.l_ref.c_ref.z_ref, bf16[256,8576]{1,0:T(8,128)(2,1)} %bitcast.2.x_ref.b_ref.l_ref.c_ref.z_ref, bf16[256,8576]{1,0:T(8,128)(2,1)} %bitcast.2.x_ref.b_ref.l_ref.c_ref.z_ref, f32[8,256,8]{2,1,0:T(8,128)S(1)} %copy.15.cum_ref, ...), custom_call_target="tpu_custom_call" | custom-call | flops 1073741824 | bytes 41943040 | tf_op jit(solution)/shard_map/inner_part/pallas_call | solution.py:172
  124.3 2.0 copy-done
  126.3 11.8 %all-to-all-done.2.state_ref = bf16[8,128,512]{2,1,0:T(8,128)(2,1)S(1)} async-done(((bf16[8,128,512]{2,1,0:T(8,128)(2,1)}), bf16[8,128,512]{2,1,0:T(8,128)(2,1)S(1)}, u32[]{:S(2)}, u32[]{:S(2)}) %all-to-all-start.2) | async-done | bytes 1048608 | tf_op jit(solution)/shard_map/all_to_all | solution.py:330
  138.1 1.1 collective-permute-start.3
  139.3 3.6 %gated_norm.2 = bf16[128,4096]{1,0:T(8,128)(2,1)S(1)} custom-call(f32[256,4096]{1,0:T(8,128)} %copy-done, bf16[256,8576]{1,0:T(8,128)(2,1)} %bitcast.2.x_ref.b_ref.l_ref.c_ref.z_ref, bf16[256,8576]{1,0:T(8,128)(2,1)} %bitcast.2.x_ref.b_ref.l_ref.c_ref.z_ref, f32[256,64]{1,0:T(8,128)S(1)} %get-tuple-element.15.cum_ref, ...), custom_call_target="tpu_custom_call" | custom-call | flops 134217728 | bytes 8388608 | tf_op jit(solution)/shard_map/gated_norm/pallas_call | solution.py:248
  143.0 4.0 %gated_norm.3 = bf16[128,4096]{1,0:T(8,128)(2,1)S(1)} custom-call(f32[256,4096]{1,0:T(8,128)} %copy-done, bf16[256,8576]{1,0:T(8,128)(2,1)} %bitcast.2.x_ref.b_ref.l_ref.c_ref.z_ref, bf16[256,8576]{1,0:T(8,128)(2,1)} %bitcast.2.x_ref.b_ref.l_ref.c_ref.z_ref, f32[256,64]{1,0:T(8,128)S(1)} %get-tuple-element.15.cum_ref, ...), custom_call_target="tpu_custom_call" | custom-call | flops 134217728 | bytes 8388608 | tf_op jit(solution)/shard_map/gated_norm/pallas_call | solution.py:248
  147.0 3.0 %collective-permute-start.8 = (bf16[128,4096]{1,0:T(8,128)(2,1)S(1)}, bf16[128,4096]{1,0:T(8,128)(2,1)S(1)}, u32[]{:S(2)}, u32[]{:S(2)}) collective-permute-start(bf16[128,4096]{1,0:T(8,128)(2,1)S(1)} %gated_norm.3), channel_id=1, source_target_pairs={{0,4},{1,5},{2,6},{3,7},{4,0},{5,1},{6,2},{7,3},{8,12},{9,13},{10,... | collective-permute-start | bytes 3145736 | tf_op jit(solution)/shard_map/ppermute | solution.py:21
  150.0 0.2 broadcast_in_dim.42
  150.2 0.7 fusion.1
  151.0 2.3 fusion.3
  153.3 0.7 fusion.5
  154.0 2.3 fusion.7
  156.3 16.4 %collective-permute-done.2 = bf16[4096,256]{1,0:T(8,128)(2,1)} collective-permute-done((bf16[4096,256]{1,0:T(8,128)(2,1)}, bf16[4096,256]{1,0:T(8,128)(2,1)}, u32[]{:S(2)}, u32[]{:S(2)}) %collective-permute-start.2) | collective-permute-done | bytes 2097184 | tf_op jit(solution)/shard_map/ppermute | solution.py:21
  172.6 2.3 fusion.9
  174.9 34.4 %collective-permute-done.4 = bf16[4096,256]{1,0:T(8,128)(2,1)} collective-permute-done((bf16[4096,256]{1,0:T(8,128)(2,1)}, bf16[4096,256]{1,0:T(8,128)(2,1)}, u32[]{:S(2)}, u32[]{:S(2)}) %collective-permute-start.4) | collective-permute-done | bytes 2097184 | tf_op jit(solution)/shard_map/ppermute | solution.py:21
  209.4 2.5 collective-permute-start.5
  211.9 2.0 fusion.19
  213.9 2.0 fusion.17
  216.0 0.4 fusion.18
  216.4 0.4 fusion.16
  217.0 26.0 %collective-permute-done.8 = bf16[128,4096]{1,0:T(8,128)(2,1)S(1)} collective-permute-done((bf16[128,4096]{1,0:T(8,128)(2,1)S(1)}, bf16[128,4096]{1,0:T(8,128)(2,1)S(1)}, u32[]{:S(2)}, u32[]{:S(2)}) %collective-permute-start.8) | collective-permute-done | bytes 1048608 | tf_op jit(solution)/shard_map/ppermute | solution.py:21
  243.0 2.1 fusion.23
  245.1 2.1 fusion.21
  247.2 0.4 fusion.22
  247.6 0.4 fusion.20
  248.2 2.0 fusion.26
  250.2 2.0 fusion.24
  252.3 2.1 fusion.29
  254.3 2.1 fusion.27
  256.4 0.4 fusion.25
  256.9 3.0 %collective-permute-start.10 = (bf16[3,128,256]{2,1,0:T(8,128)(2,1)S(1)}, bf16[3,128,256]{2,1,0:T(8,128)(2,1)S(1)}, u32[]{:S(2)}, u32[]{:S(2)}) collective-permute-start(bf16[3,128,256]{2,1,0:T(8,128)(2,1)S(1)} %pad_maximum_fusion.3), channel_id=1, source_target_pairs={{0,4},{1,5},{2,6},{3,7},{4,0},{5,1},{6,2},{7,3},{8,12},{9,13},{10,... | collective-permute-start | bytes 589832 | tf_op jit(solution)/shard_map/ppermute | solution.py:21
  259.9 0.5 fusion.28
  260.5 0.7 fusion.11
  261.2 2.3 fusion.13
  263.5 0.4 fusion.31
  264.0 0.5 fusion.30
  264.5 3.0 %collective-permute-start.12 = (bf16[2,128,256]{2,1,0:T(8,128)(2,1)S(1)}, bf16[2,128,256]{2,1,0:T(8,128)(2,1)S(1)}, u32[]{:S(2)}, u32[]{:S(2)}) collective-permute-start(bf16[2,128,256]{2,1,0:T(8,128)(2,1)S(1)} %pad_maximum_fusion.5), channel_id=1, source_target_pairs={{0,4},{1,5},{2,6},{3,7},{4,0},{5,1},{6,2},{7,3},{8,12},{9,13},{10,... | collective-permute-start | bytes 393224 | tf_op jit(solution)/shard_map/ppermute | solution.py:21
  267.5 0.7 fusion.15
  268.3 1.2 collective-permute-done.9
  269.6 5.5 %collective-permute-done.10 = bf16[3,128,256]{2,1,0:T(8,128)(2,1)S(1)} collective-permute-done((bf16[3,128,256]{2,1,0:T(8,128)(2,1)S(1)}, bf16[3,128,256]{2,1,0:T(8,128)(2,1)S(1)}, u32[]{:S(2)}, u32[]{:S(2)}) %collective-permute-start.10) | collective-permute-done | bytes 196640 | tf_op jit(solution)/shard_map/ppermute | solution.py:21
  275.2 4.2 %collective-permute-done.11 = bf16[3,128,256]{2,1,0:T(8,128)(2,1)S(1)} collective-permute-done((bf16[3,128,256]{2,1,0:T(8,128)(2,1)S(1)}, bf16[3,128,256]{2,1,0:T(8,128)(2,1)S(1)}, u32[]{:S(2)}, u32[]{:S(2)}) %collective-permute-start.11) | collective-permute-done | bytes 196640 | tf_op jit(solution)/shard_map/ppermute | solution.py:21
  279.4 1.5 collective-permute-done.12
  280.9 1.3 copy-done.5
  282.3 0.6 slice_dynamic-update-slice_fusion
  (43 shorter events, 0.9 us)
Async XLA Ops:
  2.7 1.6 copy-start.1
  4.3 1.6 copy-start.2
  9.0 59.5 %all-to-all-start = ((bf16[4,64,8576]{2,1,0:T(8,128)(2,1)}), bf16[4,64,8576]{2,1,0:T(8,128)(2,1)}, u32[]{:S(2)}, u32[]{:S(2)}) async-start(bf16[4,64,8576]{2,1,0:T(8,128)(2,1)} %bitcast.119), calls=%async_computation | async-start | bytes 8781824 | tf_op jit(solution)/shard_map/all_to_all | solution.py:295
  17.7 49.3 %collective-permute-start = (bf16[4096,256]{1,0:T(8,128)(2,1)S(1)}, bf16[4096,256]{1,0:T(8,128)(2,1)}, u32[]{:S(2)}, u32[]{:S(2)}) collective-permute-start(bf16[4096,256]{1,0:T(8,128)(2,1)S(1)} %get-tuple-element.24), channel_id=1, source_target_pairs={{0,1},{1,0},{2,3},{3,2},{4,5},{5,4},{6,7},{7,6},{8,9},{9,8},{10,11... | collective-permute-start | bytes 6291464 | tf_op jit(solution)/shard_map/ppermute | solution.py:21
  20.7 47.8 %collective-permute-start.1 = (bf16[4096,256]{1,0:T(8,128)(2,1)S(1)}, bf16[4096,256]{1,0:T(8,128)(2,1)}, u32[]{:S(2)}, u32[]{:S(2)}) collective-permute-start(bf16[4096,256]{1,0:T(8,128)(2,1)S(1)} %get-tuple-element.24), channel_id=1, source_target_pairs={{0,2},{1,3},{2,0},{3,1},{4,6},{5,7},{6,4},{7,5},{8,10},{9,11},{10,... | collective-permute-start | bytes 6291464 | tf_op jit(solution)/shard_map/ppermute | solution.py:21
  108.0 8.3 %copy-start.6 = (f32[1,64]{1,0:T(1,128)S(1)}, f32[1,64]{1,0:T(1,128)}, u32[]{:S(2)}) copy-start(f32[1,64]{1,0:T(1,128)} %param.17) | copy-start | bytes 772
  109.3 28.8 %all-to-all-start.2 = ((bf16[8,128,512]{2,1,0:T(8,128)(2,1)}), bf16[8,128,512]{2,1,0:T(8,128)(2,1)S(1)}, u32[]{:S(2)}, u32[]{:S(2)}) async-start(bf16[8,128,512]{2,1,0:T(8,128)(2,1)} %prefix_states.1), calls=%async_computation.2 | async-start | bytes 2097152 | tf_op jit(solution)/shard_map/all_to_all | solution.py:330
  112.9 59.8 %collective-permute-start.2 = (bf16[4096,256]{1,0:T(8,128)(2,1)}, bf16[4096,256]{1,0:T(8,128)(2,1)}, u32[]{:S(2)}, u32[]{:S(2)}) collective-permute-start(bf16[4096,256]{1,0:T(8,128)(2,1)} %collective-permute-done.1), channel_id=1, source_target_pairs={{0,1},{1,0},{2,3},{3,2},{4,5},{5,4},{6,7},{7,6},{8,9},{9,8},{10,11... | collective-permute-start | bytes 6291464 | tf_op jit(solution)/shard_map/ppermute | solution.py:21
  114.8 94.6 %collective-permute-start.4 = (bf16[4096,256]{1,0:T(8,128)(2,1)}, bf16[4096,256]{1,0:T(8,128)(2,1)}, u32[]{:S(2)}, u32[]{:S(2)}) collective-permute-start(bf16[4096,256]{1,0:T(8,128)(2,1)} %get-tuple-element.22), channel_id=1, source_target_pairs={{0,2},{1,3},{2,0},{3,1},{4,6},{5,7},{6,4},{7,5},{8,10},{9,11},{10,... | collective-permute-start | bytes 6291464 | tf_op jit(solution)/shard_map/ppermute | solution.py:21
  116.9 22.3 %copy-start.3 = (f32[1,4096]{1,0:T(1,128)S(1)}, f32[1,4096]{1,0:T(1,128)}, u32[]{:S(2)}) copy-start(f32[1,4096]{1,0:T(1,128)} %gain_ref.3) | copy-start | bytes 49156
  124.3 2.0 copy-start
  138.1 118.3 %collective-permute-start.3 = (bf16[4096,256]{1,0:T(8,128)(2,1)}, bf16[4096,256]{1,0:T(8,128)(2,1)S(1)}, u32[]{:S(2)}, u32[]{:S(2)}) collective-permute-start(bf16[4096,256]{1,0:T(8,128)(2,1)} %get-tuple-element.22), channel_id=1, source_target_pairs={{0,1},{1,0},{2,3},{3,2},{4,5},{5,4},{6,7},{7,6},{8,9},{9,8},{10,11... | collective-permute-start | bytes 6291464 | tf_op jit(solution)/shard_map/ppermute | solution.py:21
  142.9 69.0 %collective-permute-start.6 = (bf16[128,4096]{1,0:T(8,128)(2,1)S(1)}, bf16[128,4096]{1,0:T(8,128)(2,1)S(1)}, u32[]{:S(2)}, u32[]{:S(2)}) collective-permute-start(bf16[128,4096]{1,0:T(8,128)(2,1)S(1)} %gated_norm.2), channel_id=1, source_target_pairs={{0,4},{1,5},{2,6},{3,7},{4,0},{5,1},{6,2},{7,3},{8,12},{9,13},{10,... | collective-permute-start | bytes 3145736 | tf_op jit(solution)/shard_map/ppermute | solution.py:21
  143.0 7.2 %copy-start.4 = (bf16[1,4096,512]{2,1,0:T(8,128)(2,1)S(1)}, bf16[1,4096,512]{2,1,0:T(8,128)(2,1)}, u32[]{:S(2)}) copy-start(bf16[1,4096,512]{2,1,0:T(8,128)(2,1)} %param.15) | copy-start | bytes 12582916
  147.0 96.0 %collective-permute-start.8 = (bf16[128,4096]{1,0:T(8,128)(2,1)S(1)}, bf16[128,4096]{1,0:T(8,128)(2,1)S(1)}, u32[]{:S(2)}, u32[]{:S(2)}) collective-permute-start(bf16[128,4096]{1,0:T(8,128)(2,1)S(1)} %gated_norm.3), channel_id=1, source_target_pairs={{0,4},{1,5},{2,6},{3,7},{4,0},{5,1},{6,2},{7,3},{8,12},{9,13},{10,... | collective-permute-start | bytes 3145736 | tf_op jit(solution)/shard_map/ppermute | solution.py:21
  209.4 54.1 %collective-permute-start.5 = (bf16[4096,256]{1,0:T(8,128)(2,1)}, bf16[4096,256]{1,0:T(8,128)(2,1)S(1)}, u32[]{:S(2)}, u32[]{:S(2)}) collective-permute-start(bf16[4096,256]{1,0:T(8,128)(2,1)} %collective-permute-done.4), channel_id=1, source_target_pairs={{0,1},{1,0},{2,3},{3,2},{4,5},{5,4},{6,7},{7,6},{8,9},{9,8},{10,11... | collective-permute-start | bytes 6291464 | tf_op jit(solution)/shard_map/ppermute | solution.py:21
  216.9 51.3 %collective-permute-start.7 = (bf16[4,128,256]{2,1,0:T(8,128)(2,1)S(1)}, bf16[4,128,256]{2,1,0:T(8,128)(2,1)S(1)}, u32[]{:S(2)}, u32[]{:S(2)}) collective-permute-start(bf16[4,128,256]{2,1,0:T(8,128)(2,1)S(1)} %pad_maximum_fusion.1), channel_id=1, source_target_pairs={{0,4},{1,5},{2,6},{3,7},{4,0},{5,1},{6,2},{7,3},{8,12},{9,13},{10,... | collective-permute-start | bytes 786440 | tf_op jit(solution)/shard_map/ppermute | solution.py:21
  248.1 21.4 %collective-permute-start.9 = (bf16[4,128,256]{2,1,0:T(8,128)(2,1)S(1)}, bf16[4,128,256]{2,1,0:T(8,128)(2,1)S(1)}, u32[]{:S(2)}, u32[]{:S(2)}) collective-permute-start(bf16[4,128,256]{2,1,0:T(8,128)(2,1)S(1)} %pad_maximum_fusion.2), channel_id=1, source_target_pairs={{0,4},{1,5},{2,6},{3,7},{4,0},{5,1},{6,2},{7,3},{8,12},{9,13},{10,... | collective-permute-start | bytes 786440 | tf_op jit(solution)/shard_map/ppermute | solution.py:21
  256.9 18.2 %collective-permute-start.10 = (bf16[3,128,256]{2,1,0:T(8,128)(2,1)S(1)}, bf16[3,128,256]{2,1,0:T(8,128)(2,1)S(1)}, u32[]{:S(2)}, u32[]{:S(2)}) collective-permute-start(bf16[3,128,256]{2,1,0:T(8,128)(2,1)S(1)} %pad_maximum_fusion.3), channel_id=1, source_target_pairs={{0,4},{1,5},{2,6},{3,7},{4,0},{5,1},{6,2},{7,3},{8,12},{9,13},{10,... | collective-permute-start | bytes 589832 | tf_op jit(solution)/shard_map/ppermute | solution.py:21
  260.4 18.9 %collective-permute-start.11 = (bf16[3,128,256]{2,1,0:T(8,128)(2,1)S(1)}, bf16[3,128,256]{2,1,0:T(8,128)(2,1)S(1)}, u32[]{:S(2)}, u32[]{:S(2)}) collective-permute-start(bf16[3,128,256]{2,1,0:T(8,128)(2,1)S(1)} %pad_maximum_fusion.4), channel_id=1, source_target_pairs={{0,4},{1,5},{2,6},{3,7},{4,0},{5,1},{6,2},{7,3},{8,12},{9,13},{10,... | collective-permute-start | bytes 589832 | tf_op jit(solution)/shard_map/ppermute | solution.py:21
  264.5 16.4 %collective-permute-start.12 = (bf16[2,128,256]{2,1,0:T(8,128)(2,1)S(1)}, bf16[2,128,256]{2,1,0:T(8,128)(2,1)S(1)}, u32[]{:S(2)}, u32[]{:S(2)}) collective-permute-start(bf16[2,128,256]{2,1,0:T(8,128)(2,1)S(1)} %pad_maximum_fusion.5), channel_id=1, source_target_pairs={{0,4},{1,5},{2,6},{3,7},{4,0},{5,1},{6,2},{7,3},{8,12},{9,13},{10,... | collective-permute-start | bytes 393224 | tf_op jit(solution)/shard_map/ppermute | solution.py:21
  280.9 1.3 copy-start.5
